TPU v7x, 128 devices: a whole 4x4x4 slice. The times are simulated.
128 devices in a mesh: rows: 16 (over y, x), cols: 8 (over z, core).
Axes of the slice: x: 4, y: 4, z: 4, core: 2. Of those that a mesh axis runs over, the one named last changes fastest.
Arguments:
- embeddings: bfloat16 [12288, 1024], P('rows'), may hold values from -6 to 6
- landmarks: bfloat16 [8192, 1024], P('cols', 'rows'), may hold values from -6 to 6
- factor_rows: bfloat16 [8192, 16, 512], P('cols', None, 'rows'), may hold values from -0.0625 to 0.0625
- diag_inverse: bfloat16 [16, 512, 512], P('cols'), as said below
Outputs:
- features: bfloat16 [12288, 8192], P('rows', 'cols')
Inputs may be any that keep to these rules, and one draw needn't show every extreme that they name: `diag_inverse`: each block is lower triangular with a positive diagonal.
All inputs are finite; a program needn't handle non-finite values.
Results may differ from a plain program's by a relative error of at most 0.011.
Values may be sent and summed in bfloat16 or wider, within the bound.
No kernel may reach another device: no remote copies, remote signals or barrier semaphores. Data moves between devices by JAX's collectives and lax.ppermute only.
A program may use at most 128 MiB of HBM per device.

v0:
```python
import math

import jax
import jax.numpy as jnp
from jax import lax
from jax.sharding import PartitionSpec as P


def as_sent(shard):
    return jax.tree.map(lambda a: a.astype(jnp.bfloat16) if a.dtype == jnp.float32 else a, shard)


def broadcast(shard, axis, root):
    mine = lax.axis_index(axis) == root
    return lax.psum(jnp.where(mine, shard, jnp.zeros_like(shard)), axis)


def kernel_terms(piece, embeddings):
    return lax.dot_general(
        embeddings, piece, (((1,), (1,)), ((), ())), preferred_element_type=jnp.float32
    )


def finalize(running, own_slice, diag_inverse):
    width = diag_inverse.shape[1]
    count = diag_inverse.shape[0]
    solved_list = []
    for column in range(count):
        current = running[:, column * width : (column + 1) * width]
        for earlier in range(column):
            factor_block = own_slice[column * width : (column + 1) * width, earlier, :]
            current = current - lax.dot_general(
                solved_list[earlier],
                factor_block,
                (((1,), (1,)), ((), ())),
                preferred_element_type=jnp.float32,
            )
        rounded = current.astype(jnp.bfloat16)
        product = lax.dot_general(
            rounded,
            diag_inverse[column],
            (((1,), (1,)), ((), ())),
            preferred_element_type=jnp.float32,
        )
        solved_list.append(product.astype(jnp.bfloat16))
    return jnp.concatenate(solved_list, axis=1)


def subtract_update(running, arrived, own_slice):
    flat = own_slice.reshape(own_slice.shape[0], -1)
    return running - lax.dot_general(
        arrived, flat, (((1,), (1,)), ((), ())), preferred_element_type=jnp.float32
    )


def per_device(embeddings, landmarks, factor_rows, diag_inverse):
    blocks_own = diag_inverse.shape[0]
    block_size = diag_inverse.shape[1]
    col_count = lax.axis_size("cols")
    my_index = lax.axis_index("cols")
    scores = kernel_terms(lax.all_gather(landmarks, "rows", axis=1, tiled=True), embeddings)
    scale = 0.5 / math.sqrt(embeddings.shape[1])
    running = jnp.exp(scores * scale)
    whole_panel = lax.all_gather(factor_rows, "rows", axis=2, tiled=True)

    def fetch(turn):
        return lax.dynamic_slice_in_dim(whole_panel, turn * blocks_own, blocks_own, 1)

    solved = jnp.zeros((embeddings.shape[0], blocks_own * block_size), jnp.bfloat16)

    def advance(turn, carry):
        running, solved = carry
        own_slice = fetch(turn)
        solved = lax.cond(
            my_index == turn, lambda: finalize(running, own_slice, diag_inverse), lambda: solved
        )
        arrived = broadcast(as_sent(solved), "cols", turn).astype(solved.dtype)
        running = lax.cond(
            my_index > turn, lambda: subtract_update(running, arrived, own_slice), lambda: running
        )
        return (running, solved)

    running, solved = lax.fori_loop(0, col_count - 1, advance, (running, solved))
    last_slice = fetch(col_count - 1)
    solved = lax.cond(
        my_index == col_count - 1,
        lambda: finalize(running, last_slice, diag_inverse),
        lambda: solved,
    )
    return solved


def solution(mesh):
    in_specs = (P("rows", None), P("cols", "rows"), P("cols", None, "rows"), P("cols", None, None))
    out_specs = P("rows", "cols")
    return jax.shard_map(
        per_device, mesh=mesh, in_specs=in_specs, out_specs=out_specs, check_vma=False
    )
```

profile of v0, /device:TPU:97, one launch (start us, length us, event | category | flops | bytes accessed | tf_op | source)
XLA Modules:
  0.0 890.8 jit_solution(9188046008652768149)
XLA Ops:
  7.3 2.8 copy.17
  10.1 44.7 %all-gather.3.cloned.1.call-done = bf16[1024,1024]{0,1:T(8,128)(2,1)} async-done(((bf16[1024,64]{0,1:T(8,128)(2,1)}), bf16[1024,1024]{0,1:T(8,128)(2,1)}) %all-gather.3.cloned.1.call-update) | async-done | bytes 2097168 | tf_op jit(solution)/shard_map/all_gather | solution.py:61
  54.8 5.0 multiply_exponential_fusion
  59.8 108.5 %all-gather.5.cloned.1.call-done = bf16[1024,16,512]{0,1,2:T(8,128)(2,1)} async-done(((bf16[1024,16,32]{0,1,2:T(8,128)(2,1)}), bf16[1024,16,512]{0,1,2:T(8,128)(2,1)}) %all-gather.5.cloned.1.call-update) | async-done | bytes 16777232 | tf_op jit(solution)/shard_map/all_gather | solution.py:64
  168.3 1.3 broadcast.10
  169.6 680.4 %while.24 = (s32[]{:T(128)}, f32[768,1024]{1,0:T(8,128)}, bf16[768,1024]{0,1:T(8,128)(2,1)}, s32[]{:T(128)}, bf16[1024,16,512]{0,1,2:T(8,128)(2,1)}, /*index=5*/...) while((s32[]{:T(128)}, f32[768,1024]{1,0:T(8,128)}, ...), condition=%wide.region_6.7_spmd, body=%wide.region_0.6_spmd.sunk | while | flops 2825650176 | bytes 66584988 | solution.py:83
  169.6 6.9 constant_dynamic-slice_fusion.2
  176.6 8.6 copy.25
  185.2 1.7 copy.26
  186.9 1.2 broadcast_select_fusion.2
  188.2 70.2 %all-reduce.2.cloned.1.call-done = bf16[768,1024]{1,0:T(8,128)(2,1)} async-done(((bf16[768,1024]{1,0:T(8,128)(2,1)}), bf16[768,1024]{1,0:T(8,128)(2,1)}) %all-reduce.2.cloned.1.call-update) | async-done | bytes 1572880 | tf_op jit(solution)/shard_map/while/body/eval_jaxpr/psum | solution.py:15
  258.4 7.7 conditional.7
  258.4 2.3 copy.22
  260.7 5.4 convolution_subtract_fusion
  266.1 6.9 constant_dynamic-slice_fusion.2
  273.0 8.6 copy.25
  281.6 1.7 copy.26
  284.6 70.4 %all-reduce.2.cloned.1.call-done = bf16[768,1024]{1,0:T(8,128)(2,1)} async-done(((bf16[768,1024]{1,0:T(8,128)(2,1)}), bf16[768,1024]{1,0:T(8,128)(2,1)}) %all-reduce.2.cloned.1.call-update) | async-done | bytes 1572880 | tf_op jit(solution)/shard_map/while/body/eval_jaxpr/psum | solution.py:15
  355.0 7.7 conditional.7
  355.0 2.3 copy.22
  357.3 5.4 convolution_subtract_fusion
  362.7 6.9 constant_dynamic-slice_fusion.2
  369.6 8.6 copy.25
  378.3 1.7 copy.26
  380.0 1.2 broadcast_select_fusion.2
  381.3 71.5 %all-reduce.2.cloned.1.call-done = bf16[768,1024]{1,0:T(8,128)(2,1)} async-done(((bf16[768,1024]{1,0:T(8,128)(2,1)}), bf16[768,1024]{1,0:T(8,128)(2,1)}) %all-reduce.2.cloned.1.call-update) | async-done | bytes 1572880 | tf_op jit(solution)/shard_map/while/body/eval_jaxpr/psum | solution.py:15
  452.8 7.7 conditional.7
  452.8 2.3 copy.22
  455.1 5.4 convolution_subtract_fusion
  460.5 6.9 constant_dynamic-slice_fusion.2
  467.4 8.6 copy.25
  476.0 1.7 copy.26
  479.0 69.2 %all-reduce.2.cloned.1.call-done = bf16[768,1024]{1,0:T(8,128)(2,1)} async-done(((bf16[768,1024]{1,0:T(8,128)(2,1)}), bf16[768,1024]{1,0:T(8,128)(2,1)}) %all-reduce.2.cloned.1.call-update) | async-done | bytes 1572880 | tf_op jit(solution)/shard_map/while/body/eval_jaxpr/psum | solution.py:15
  548.2 7.7 conditional.7
  548.2 2.3 copy.22
  550.5 5.4 convolution_subtract_fusion
  555.9 6.9 constant_dynamic-slice_fusion.2
  562.8 8.6 copy.25
  571.5 1.7 copy.26
  573.2 1.2 broadcast_select_fusion.2
  574.4 71.2 %all-reduce.2.cloned.1.call-done = bf16[768,1024]{1,0:T(8,128)(2,1)} async-done(((bf16[768,1024]{1,0:T(8,128)(2,1)}), bf16[768,1024]{1,0:T(8,128)(2,1)}) %all-reduce.2.cloned.1.call-update) | async-done | bytes 1572880 | tf_op jit(solution)/shard_map/while/body/eval_jaxpr/psum | solution.py:15
  645.7 7.7 conditional.7
  645.7 2.3 copy.22
  648.0 5.4 convolution_subtract_fusion
  653.4 6.9 constant_dynamic-slice_fusion.2
  660.3 8.6 copy.25
  668.9 1.7 copy.26
  671.9 71.5 %all-reduce.2.cloned.1.call-done = bf16[768,1024]{1,0:T(8,128)(2,1)} async-done(((bf16[768,1024]{1,0:T(8,128)(2,1)}), bf16[768,1024]{1,0:T(8,128)(2,1)}) %all-reduce.2.cloned.1.call-update) | async-done | bytes 1572880 | tf_op jit(solution)/shard_map/while/body/eval_jaxpr/psum | solution.py:15
  743.4 7.7 conditional.7
  743.4 2.3 copy.22
  745.7 5.4 convolution_subtract_fusion
  751.1 6.9 constant_dynamic-slice_fusion.2
  758.0 8.6 copy.25
  766.7 1.7 copy.26
  769.7 72.7 %all-reduce.2.cloned.1.call-done = bf16[768,1024]{1,0:T(8,128)(2,1)} async-done(((bf16[768,1024]{1,0:T(8,128)(2,1)}), bf16[768,1024]{1,0:T(8,128)(2,1)}) %all-reduce.2.cloned.1.call-update) | async-done | bytes 1572880 | tf_op jit(solution)/shard_map/while/body/eval_jaxpr/psum | solution.py:15
  842.3 7.7 conditional.7
  842.3 2.3 copy.22
  844.7 5.4 convolution_subtract_fusion
  850.0 31.6 %conditional.3 = (bf16[768,1024]{0,1:T(8,128)(2,1)}) conditional(s32[]{:T(128)} %convert_element_type.37, bf16[768,1024]{0,1:T(8,128)(2,1)} %get-tuple-element.282, (f32[768,1024]{1,0:T(8,128)}, bf16[2,512,512]{2,1,0:T(8,128)(2,1)S(1)}, bf16[1024,16,512]{0,1,2:T(8,128)(2,1)}) %tuple.86), branch_computations={%region_7.8_spmd, %region_8.9_spmd} | conditional | flops 1212678144 | bytes 42991624 | solution.py:85
  850.0 23.6 %copy.19 = bf16[1024,16,512]{2,0,1:T(8,128)(2,1)} copy(bf16[1024,16,512]{0,1,2:T(8,128)(2,1)} %get-tuple-element.186) | data formatting | bytes 33554432 | tf_op jit(solution)/shard_map
  873.7 2.0 convolution_convert_fusion.3
  875.7 3.6 convolution_convert_fusion.2
  879.3 2.4 pad_maximum_fusion.1
  881.7 2.6 copy.20
  (61 shorter events, 6.0 us)
Async XLA Ops:
  6.5 48.3 %copy-start = (bf16[768,1024]{1,0:T(8,128)(2,1)S(1)}, bf16[768,1024]{1,0:T(8,128)(2,1)}, u32[]{:S(2)}) copy-start(bf16[768,1024]{1,0:T(8,128)(2,1)} %param.12) | copy-start | bytes 4718596
  6.5 48.2 %all-gather.3.cloned.1.call-start = ((), (), s32[]{:S(2)}) async-start(), calls=%async_computation | async-start | bytes 2228224 | tf_op jit(solution)/shard_map/all_gather | solution.py:61
  7.3 161.1 %all-gather.5.cloned.1.call-start = ((), (), s32[]{:S(2)}) async-start(), calls=%async_computation.1 | async-start | bytes 17825792 | tf_op jit(solution)/shard_map/all_gather | solution.py:64
  10.1 159.5 %copy-start.1 = (bf16[2,512,512]{2,1,0:T(8,128)(2,1)S(1)}, bf16[2,512,512]{2,1,0:T(8,128)(2,1)}, u32[]{:S(2)}) copy-start(bf16[2,512,512]{2,1,0:T(8,128)(2,1)} %param.15) | copy-start | bytes 3145732
  169.6 88.7 %all-reduce.2.cloned.1.call-start = ((), (), s32[]{:S(2)}) async-start(), calls=%async_computation.2 | async-start | bytes 3145728 | tf_op jit(solution)/shard_map/while/body/eval_jaxpr/psum | solution.py:15
  258.4 7.7 copy-start.2
  258.4 2.3 copy-start.4
  266.1 88.9 %all-reduce.2.cloned.1.call-start = ((), (), s32[]{:S(2)}) async-start(), calls=%async_computation.2 | async-start | bytes 3145728 | tf_op jit(solution)/shard_map/while/body/eval_jaxpr/psum | solution.py:15
  355.0 7.7 copy-start.2
  355.0 2.3 copy-start.4
  362.7 90.0 %all-reduce.2.cloned.1.call-start = ((), (), s32[]{:S(2)}) async-start(), calls=%async_computation.2 | async-start | bytes 3145728 | tf_op jit(solution)/shard_map/while/body/eval_jaxpr/psum | solution.py:15
  452.8 7.7 copy-start.2
  452.8 2.3 copy-start.4
  460.5 87.7 %all-reduce.2.cloned.1.call-start = ((), (), s32[]{:S(2)}) async-start(), calls=%async_computation.2 | async-start | bytes 3145728 | tf_op jit(solution)/shard_map/while/body/eval_jaxpr/psum | solution.py:15
  548.2 7.7 copy-start.2
  548.2 2.3 copy-start.4
  555.9 89.8 %all-reduce.2.cloned.1.call-start = ((), (), s32[]{:S(2)}) async-start(), calls=%async_computation.2 | async-start | bytes 3145728 | tf_op jit(solution)/shard_map/while/body/eval_jaxpr/psum | solution.py:15
  645.7 7.7 copy-start.2
  645.7 2.3 copy-start.4
  653.4 90.0 %all-reduce.2.cloned.1.call-start = ((), (), s32[]{:S(2)}) async-start(), calls=%async_computation.2 | async-start | bytes 3145728 | tf_op jit(solution)/shard_map/while/body/eval_jaxpr/psum | solution.py:15
  743.4 7.7 copy-start.2
  743.4 2.3 copy-start.4
  751.1 91.2 %all-reduce.2.cloned.1.call-start = ((), (), s32[]{:S(2)}) async-start(), calls=%async_computation.2 | async-start | bytes 3145728 | tf_op jit(solution)/shard_map/while/body/eval_jaxpr/psum | solution.py:15
  842.3 7.7 copy-start.2
  842.3 2.3 copy-start.4
Sparse Core Ops, SparseCore 0:
  9.5 45.2 all-gather.2
  56.9 111.3 all-gather.4
  188.3 70.0 all-reduce.1
  284.7 70.2 all-reduce.1
  381.4 71.3 all-reduce.1
  479.1 69.0 all-reduce.1
  574.6 71.0 all-reduce.1
  672.0 71.3 all-reduce.1
  769.8 72.5 all-reduce.1
where the time goes:
time: 894 us; the launch traced here: 891 us
  waiting for transfers between devices  651 us (73%)
  local copies, waits for them, and re-layouts  167 us (19%)
  matrix products  48.3 us (5%)
  between operations  13.1 us (1%)
  other arithmetic  11.2 us (1%)
    psum x7, waiting for transfers between devices, broadcast(): return lax.psum(jnp.where(mine, shard, jnp.zeros_like(shard)), axis)  497 us
    dynamic_slice x14, local copies, waits for them, and re-layouts, fetch(): lax.dynamic_slice_in_dim(whole_panel, turn * blocks_own, blocks_own, 1)  109 us
    all_gather x1, waiting for transfers between devices, per_device(): whole_panel = lax.all_gather(factor_rows, 'rows', axis=2, tiled=True)  109 us
    all_gather x1, waiting for transfers between devices, per_device(): lax.all_gather(landmarks, 'rows', axis=1, tiled=True)  44.7 us
    dot_general x7, matrix products, subtract_update(): lax.dot_general(arrived, flat, (((1,), (1,)), ((), ())), preferred_elemen...  37.6 us
    another operation x2, local copies, waits for them, and re-layouts  24.9 us
  transfers between devices with their start and end apart: 9, of which 9 were waited for; matrix products, arithmetic and copies ran while one was open for 1% of the time, Pallas kernels for 0%

commit v1 on v0

v1 whole, which is shorter than its diff:
```python
import functools
import math

import jax
import jax.numpy as jnp
from jax import lax
from jax.experimental import pallas as pl
from jax.experimental.pallas import tpu as pltpu
from jax.sharding import PartitionSpec as P

CHUNKS = 2
BF = jnp.bfloat16
F32 = jnp.float32


def mm(a, b):
    return jnp.dot(a, b, preferred_element_type=F32)


def scores_kernel(scale, info, emb, lm_own, lm_oth, out):
    core = info[1]
    depth = emb.shape[1]
    width = lm_own.shape[2]
    for slot, lm in ((core, lm_own), (1 - core, lm_oth)):
        points = lm[...].reshape(depth, width)
        out[0, pl.ds(slot, 1)] = jnp.exp(mm(emb[...], points) * scale)[None]


def solve(running, even, odd, dt_even, dt_odd, store):
    size = dt_even.shape[1]
    r0, r1, r2, r3 = (running[i // 2, :, (i % 2) * size:(i % 2 + 1) * size] for i in range(4))
    l10 = even[:, 0:32, 0:size].reshape(size, size)
    l32 = even[:, 0:32, size:].reshape(size, size)
    l20 = odd[:, 0:32, 0:size].reshape(size, size)
    l30 = odd[:, 0:32, size:].reshape(size, size)
    l21 = odd[:, 32:64, 0:size].reshape(size, size)
    l31 = odd[:, 32:64, size:].reshape(size, size)
    f0 = mm(r0.astype(BF), dt_even[0]).astype(BF)
    store(0, f0)
    r1 = r1 - mm(f0, l10)
    f1 = mm(r1.astype(BF), dt_even[1]).astype(BF)
    store(1, f1)
    r2 = r2 - mm(f0, l20) - mm(f1, l21)
    f2 = mm(r2.astype(BF), dt_odd[0]).astype(BF)
    store(2, f2)
    r3 = r3 - mm(f0, l30) - mm(f1, l31) - mm(f2, l32)
    f3 = mm(r3.astype(BF), dt_odd[1]).astype(BF)
    store(3, f3)


def finish_kernel(info, r, a, l_own, l_oth, dg_own, dg_oth, dt_own, dt_oth, every_in, f, every, acc, sem):
    step = pl.program_id(0)
    plane, core, slot, valid = info[0], info[1], info[3], info[4]
    size = a.shape[2]

    @pl.when(step == 0)
    def _():
        acc[...] = r[0]

    @pl.when((plane > 0) & (valid == 1))
    def _():
        for where, block in ((core, l_own), (1 - core, l_oth)):
            acc[pl.ds(where, 1)] -= mm(a[0], block[...].reshape(size, -1))[None]

    @pl.when((step == pl.num_programs(0) - 1) & (valid == 1))
    def _():
        def store(i, value):
            f[i // 2, :, (i % 2) * size:(i % 2 + 1) * size] = value

        @pl.when(core == 0)
        def _():
            solve(acc, dg_own, dg_oth, dt_own, dt_oth, store)

        @pl.when(core == 1)
        def _():
            solve(acc, dg_oth, dg_own, dt_oth, dt_own, store)

    @pl.when(step == pl.num_programs(0) - 1)
    def _():
        out = pltpu.make_async_copy(f, every.at[slot], sem)
        out.start()
        out.wait()


def early_kernel(info, r, own, b, c, l_own, l_oth, r_out, p, acc):
    step = pl.program_id(0)
    plane, core, valid = info[0], info[1], info[3]
    size = b.shape[2]

    @pl.when(step == 0)
    def _():
        acc[...] = jnp.zeros_like(acc)

    def add(source):
        for where, block in ((core, l_own), (1 - core, l_oth)):
            acc[pl.ds(where, 1)] += mm(source[0], block[...].reshape(size, -1))[None]

    @pl.when((valid == 1) & (plane == 0))
    def _():
        add(own)

    @pl.when((valid == 1) & (plane >= 2))
    def _():
        add(b)

    @pl.when(step == pl.num_programs(0) - 1)
    def _():
        p[...] = acc[...].astype(BF)

        @pl.when((valid == 1) & (plane == 2))
        def _():
            r_out[0] = r[0] - acc[...]

        @pl.when((valid == 1) & (plane == 3))
        def _():
            r_out[0] = r[0] - acc[...] - c[...].astype(F32)

        @pl.when((valid == 0) | (plane < 2))
        def _():
            r_out[0] = r[0]


def params():
    return pltpu.CompilerParams(dimension_semantics=("arbitrary",), vmem_limit_bytes=48 << 20)


def per_device(embeddings, landmarks, factor_rows, diag_inverse):
    tokens, depth = embeddings.shape
    rows = lax.axis_size("rows")
    planes = lax.axis_size("cols") // 2
    here = lax.axis_index("cols")
    plane, core = here // 2, here % 2
    own_rows, blocks, slab = factor_rows.shape
    size = diag_inverse.shape[1]
    n = CHUNKS
    t = tokens // 2 // n
    scale = 0.5 / math.sqrt(depth)
    per_plane = blocks // planes

    def shift(x, by, sources):
        pairs = [(2 * z + k, 2 * ((z + by) % planes) + k) for z in sources for k in range(2)]
        return lax.ppermute(x, "cols", pairs)

    def swap(x):
        return lax.ppermute(x, "cols", [(c, c ^ 1) for c in range(2 * planes)])

    ft = factor_rows.transpose(1, 2, 0)
    first = shift(ft[:per_plane], -3, [3])
    dt_own = diag_inverse.transpose(0, 2, 1)
    dt_oth = swap(dt_own)
    mine = lax.dynamic_slice_in_dim(ft, per_plane * plane, per_plane, 0)
    to_even = lax.ppermute(mine[2, :, size:], "cols", [(2 * z + 1, 2 * z) for z in range(planes)])
    even_diag = jnp.stack([jnp.concatenate([mine[0, :, size:], to_even], axis=1), mine[1]])
    diag = jnp.where(core == 0, even_diag, mine[:2])
    head = jnp.concatenate([landmarks.T, diag.reshape(2 * slab, own_rows)], axis=0)

    def gather(x):
        return lax.all_gather(x, "rows", axis=0, tiled=False)

    head_own = gather(head)
    late = gather(lax.dynamic_slice_in_dim(ft, per_plane * jnp.maximum(plane - 1, 0), per_plane, 0))
    early_shard = jnp.where(
        plane == 0, first, lax.dynamic_slice_in_dim(ft, per_plane * jnp.maximum(plane - 2, 0), per_plane, 0)
    )
    early = gather(early_shard)
    head_oth = swap(head_own)
    late_oth = swap(late)
    early_oth = swap(early)

    lead = landmarks.shape[1]
    emb = lax.dynamic_slice_in_dim(embeddings, core * (tokens // 2), tokens // 2, 0)
    where = jnp.stack([plane, core]).astype(jnp.int32)
    whole = lambda *shape: pl.BlockSpec(shape, lambda i, s: (0,) * len(shape))
    running = pl.pallas_call(
        functools.partial(scores_kernel, scale),
        grid_spec=pltpu.PrefetchScalarGridSpec(
            num_scalar_prefetch=1,
            grid=(n,),
            in_specs=[
                pl.BlockSpec((t, depth), lambda i, s: (i, 0)),
                whole(rows, lead, own_rows),
                whole(rows, lead, own_rows),
            ],
            out_specs=pl.BlockSpec((1, 2, t, own_rows), lambda i, s: (i, 0, 0, 0)),
        ),
        out_shape=jax.ShapeDtypeStruct((n, 2, t, own_rows), F32),
        compiler_params=params(),
        name="scores",
    )(where, emb, head_own, head_oth)

    f_spec = pl.BlockSpec((1, t, size), lambda k, s: (k // 2, 0, k % 2))
    l_spec = pl.BlockSpec((rows, 1, slab, own_rows), lambda k, s: (0, k, 0, 0))
    r_spec = pl.BlockSpec((1, 2, t, own_rows), lambda k, s: (s[2], 0, 0, 0))
    dg_spec = pl.BlockSpec((rows, 2 * slab, own_rows), lambda k, s: (0, lead // (2 * slab), 0))
    flops = 2 * t * per_plane * size * 2 * own_rows

    def finish(step, running, arrived, every):
        chunk = step - plane
        valid = (chunk >= 0) & (chunk < n)
        info = jnp.stack([plane, core, jnp.clip(chunk, 0, n - 1), jnp.where(valid, chunk, n), valid]).astype(jnp.int32)
        return pl.pallas_call(
            finish_kernel,
            grid_spec=pltpu.PrefetchScalarGridSpec(
                num_scalar_prefetch=1,
                grid=(per_plane,),
                in_specs=[
                    r_spec, f_spec, l_spec, l_spec, dg_spec, dg_spec,
                    whole(2, size, size), whole(2, size, size),
                    pl.BlockSpec(memory_space=pl.ANY),
                ],
                out_specs=[whole(2, t, own_rows), pl.BlockSpec(memory_space=pl.ANY)],
                scratch_shapes=[pltpu.VMEM((2, t, own_rows), F32), pltpu.SemaphoreType.DMA],
            ),
            out_shape=[
                jax.ShapeDtypeStruct((2, t, own_rows), BF),
                jax.ShapeDtypeStruct((n + 1, 2, t, own_rows), BF),
            ],
            input_output_aliases={9: 1},
            compiler_params=params(),
            cost_estimate=pl.CostEstimate(flops=flops * 2, bytes_accessed=24 << 20, transcendentals=0),
            name="finish",
        )(info, running, arrived, late, late_oth, head_own, head_oth, dt_own, dt_oth, every)

    def ahead(step, running, own, arrived, partial):
        chunk = jnp.where(plane == 0, step, step + 1 - plane)
        valid = (chunk >= 0) & (chunk < n) & (plane != 1)
        info = jnp.stack([plane, core, jnp.clip(chunk, 0, n - 1), valid]).astype(jnp.int32)
        return pl.pallas_call(
            early_kernel,
            grid_spec=pltpu.PrefetchScalarGridSpec(
                num_scalar_prefetch=1,
                grid=(per_plane,),
                in_specs=[r_spec, f_spec, f_spec, whole(2, t, own_rows), l_spec, l_spec],
                out_specs=[r_spec, whole(2, t, own_rows)],
                scratch_shapes=[pltpu.VMEM((2, t, own_rows), F32)],
            ),
            out_shape=[
                jax.ShapeDtypeStruct((n, 2, t, own_rows), F32),
                jax.ShapeDtypeStruct((2, t, own_rows), BF),
            ],
            input_output_aliases={1: 0},
            compiler_params=params(),
            cost_estimate=pl.CostEstimate(flops=flops, bytes_accessed=20 << 20, transcendentals=0),
            name="ahead",
        )(info, running, own, arrived, partial, early, early_oth)

    none = jnp.zeros((2, t, own_rows), BF)
    every = jnp.zeros((n + 1, 2, t, own_rows), BF)
    one_back = none
    two_back = none
    partials = []
    for step in range(n + planes - 1):
        f, every = finish(step, running, one_back, every)
        active = [z for z in range(planes) if 0 <= step - z < n]
        if step == n + planes - 2:
            break
        near = [z for z in active if z + 1 < planes]
        far = [z for z in active if z + 2 < planes]
        partial = partials[step - 2] if 0 <= step - 2 < len(partials) else none
        one_back = shift(f, 1, near)
        next_two = shift(f, 2, far) if far else none
        running, p = ahead(step, running, f, two_back, partial)
        if step < n:
            partials.append(shift(p, -1, [0]))
        two_back = next_two

    done = every[:n]
    keep = lax.dynamic_index_in_dim(done, core, 1, False).reshape(n * t, own_rows)
    give = lax.dynamic_index_in_dim(done, 1 - core, 1, False).reshape(n * t, own_rows)
    got = swap(give)
    return jnp.where(
        core == 0, jnp.concatenate([keep, got], axis=0), jnp.concatenate([got, keep], axis=0)
    )


def solution(mesh):
    in_specs = (P("rows", None), P("cols", "rows"), P("cols", None, "rows"), P("cols", None, None))
    out_specs = P("rows", "cols")
    return jax.shard_map(
        per_device, mesh=mesh, in_specs=in_specs, out_specs=out_specs, check_vma=False
    )
```

time: 894 us -> 334 us (0.37)
  waiting for transfers between devices: 651 us -> 197 us
  local copies, waits for them, and re-layouts: 167 us -> 17.3 us
  Pallas kernels: 0 us -> 78.5 us
  matrix products: 48.3 us -> 0 us
  starting transfers between devices: 0.06 us -> 22 us
    psum x7 -> x0, waiting for transfers between devices: 497 us -> none  [broadcast(): return lax.psum(jnp.where(mine, shard, jnp.zeros_like(shard)), axis)]
    dynamic_slice x14 -> x3, local copies, waits for them, and re-layouts: 109 us -> 2.1 us  [the longest x1 1.88 us: per_device(): lax.dynamic_slice_in_dim(ft, per_plane * jnp.maximum(plane - 1, 0), per_p...]
    pallas_call x0 -> x10, Pallas kernels: none -> 78.5 us  [the longest x5 43.9 us: finish(): pl.pallas_call(finish_kernel, grid_spec=pltpu.PrefetchScalarGridSpec(num_...]
    ppermute x0 -> x16, waiting for transfers between devices: none -> 48.7 us  [the longest x10 45.9 us: shift(): return lax.ppermute(x, 'cols', pairs)]
    dot_general x10 -> x0, matrix products: 48.3 us -> none  [the longest x7 37.6 us: subtract_update(): lax.dot_general(arrived, flat, (((1,), (1,)), ((), ())), preferred_elemen...]
    cond x28 -> x0, local copies, waits for them, and re-layouts: 28.1 us -> none
    another operation x2 -> x5, local copies, waits for them, and re-layouts: 24.9 us -> 0.43 us  [finish(): jnp.stack([plane, core, jnp.clip(chunk, 0, n - 1), jnp.where(valid, chunk...]
    ppermute x0 -> x16, starting transfers between devices: none -> 21.9 us  [the longest x10 14.2 us: shift(): return lax.ppermute(x, 'cols', pairs)]
  transfers between devices with their start and end apart: 9 -> 19, of which waited for: 9 -> 11; matrix products, arithmetic and copies ran while one was open for 1% -> 2% of each run, Pallas kernels for 0% -> 20%
where the time goes in v1:
time: 334 us; the launch traced here: 333 us
  waiting for transfers between devices  197 us (59%)
  Pallas kernels  78.5 us (24%)
  starting transfers between devices  22 us (7%)
  local copies, waits for them, and re-layouts  17.3 us (5%)
  between operations  13.5 us (4%)
  other arithmetic  5.42 us (2%)
    all_gather x3, waiting for transfers between devices, gather(): return lax.all_gather(x, 'rows', axis=0, tiled=False)  147 us
    ppermute x10, waiting for transfers between devices, shift(): return lax.ppermute(x, 'cols', pairs)  45.9 us
    pallas_call x5, Pallas kernels, finish(): pl.pallas_call(finish_kernel, grid_spec=pltpu.PrefetchScalarGridSpec(num_...  43.9 us
    pallas_call x4, Pallas kernels, ahead(): pl.pallas_call(early_kernel, grid_spec=pltpu.PrefetchScalarGridSpec(num_s...  29.6 us
    ppermute x10, starting transfers between devices, shift(): return lax.ppermute(x, 'cols', pairs)  14.2 us
    unnamed x29, local copies, waits for them, and re-layouts  13.3 us
  transfers between devices with their start and end apart: 19, of which 11 were waited for; matrix products, arithmetic and copies ran while one was open for 2% of the time, Pallas kernels for 20%

profile of v1, /device:TPU:97, one launch (start us, length us, event | category | flops | bytes accessed | tf_op | source)
XLA Modules:
  0.0 333.4 jit_solution(3899117041744796076)
XLA Ops:
  6.5 1.9 dynamic-slice_bitcast_fusion
  8.4 2.6 collective-permute-start
  11.0 0.8 collective-permute-done
  11.9 1.6 pad_maximum_fusion
  13.6 0.7 all-gather.9.cloned.1.call-update
  14.3 1.0 slice.28
  15.3 1.3 collective-permute-start.4
  16.6 5.6 %collective-permute-done.4 = bf16[4,32,1024]{2,1,0:T(8,128)(2,1)S(1)} collective-permute-done((bf16[4,32,1024]{2,1,0:T(8,128)(2,1)S(1)}, bf16[4,32,1024]{2,1,0:T(8,128)(2,1)S(1)}, u32[]{:S(2)}, u32[]{:S(2)}) %collective-permute-start.4) | collective-permute-done | bytes 262176 | tf_op jit(solution)/shard_map/ppermute | solution.py:142
  22.2 1.7 bitcast_select_fusion
  24.0 42.1 %all-gather.7.cloned.1.call-done = bf16[2048,1024]{1,0:T(8,128)(2,1)} async-done(((bf16[128,1024]{1,0:T(8,128)(2,1)}), bf16[2048,1024]{1,0:T(8,128)(2,1)}) %all-gather.7.cloned.1.call-update) | async-done | bytes 4194320 | tf_op jit(solution)/shard_map/all_gather | solution.py:158
  66.1 0.7 collective-permute-start.1
  66.7 52.6 %all-gather.9.cloned.1.call-done = bf16[64,32,1024]{2,1,0:T(8,128)(2,1)} async-done(((bf16[4,32,1024]{2,1,0:T(8,128)(2,1)}), bf16[64,32,1024]{2,1,0:T(8,128)(2,1)}) %all-gather.9.cloned.1.call-update) | async-done | bytes 4194320 | tf_op jit(solution)/shard_map/all_gather | solution.py:158
  119.3 0.7 collective-permute-start.2
  120.0 52.6 %all-gather.11.cloned.1.call-done = bf16[64,32,1024]{2,1,0:T(8,128)(2,1)} async-done(((bf16[4,32,1024]{2,1,0:T(8,128)(2,1)}), bf16[64,32,1024]{2,1,0:T(8,128)(2,1)}) %all-gather.11.cloned.1.call-update) | async-done | bytes 4194320 | tf_op jit(solution)/shard_map/all_gather | solution.py:158
  172.6 0.7 collective-permute-start.5
  173.3 1.5 copy.15
  174.8 0.1 collective-permute-start.3
  174.9 0.1 stack.186.info
  175.0 0.1 pad_add_fusion.5.info
  175.2 4.9 %scores.1.r = f32[2,2,192,1024]{3,2,1,0:T(8,128)S(1)} custom-call(s32[2]{0:T(128)S(1)} %pad_add_fusion.5.info, bf16[384,1024]{1,0:T(8,128)(2,1)S(1)} %constant_dynamic-slice_fusion.2.emb, bf16[16,128,1024]{2,1,0:T(8,128)(2,1)} %bitcast.53, bf16[16,128,1024]{2,1,0:T(8,128)(2,1)} %collective-permute-done.1.lm_oth.dg_oth), custom_call_target="tpu_custom_call" | custom-call | tf_op jit(solution)/shard_map/scores/pallas_call | solution.py:174
  180.1 1.6 copy-done.1
  181.7 0.1 collective-permute-done.3.dt_oth
  181.7 0.1 broadcast_in_dim.6.a.b.c
  181.8 0.3 broadcast_in_dim.7.every_in
  182.1 7.6 %finish.5 = (bf16[2,192,1024]{2,1,0:T(8,128)(2,1)}, bf16[3,2,192,1024]{3,2,1,0:T(8,128)(2,1)S(1)}) custom-call(s32[5]{0:T(128)S(1)} %stack.186.info, f32[2,2,192,1024]{3,2,1,0:T(8,128)} %copy-done.1, bf16[2,192,1024]{2,1,0:T(8,128)(2,1)S(1)} %broadcast_in_dim.6.a.b.c, bf16[16,4,32,1024]{3,2,1,0:T(8,128)(2,1)} %bitcast.60, ...), custom_call_target="tpu_custom_call", output_to_operand_aliasing={{1}: (9, {})} | custom-call | flops 3221225472 | bytes 25165824 | tf_op jit(solution)/shard_map/finish/pallas_call | solution.py:201
  189.7 1.4 copy-done.4
  191.1 1.6 collective-permute-start.6
  192.7 0.1 stack.191.info
  192.8 0.1 pad_add_fusion.4
  192.9 1.6 collective-permute-start.7
  194.5 1.9 copy-done.2
  196.4 5.2 %ahead.4 = (f32[2,2,192,1024]{3,2,1,0:T(8,128)S(1)}, bf16[2,192,1024]{2,1,0:T(8,128)(2,1)S(1)}) custom-call(s32[4]{0:T(128)S(1)} %get-tuple-element.35.info, f32[2,2,192,1024]{3,2,1,0:T(8,128)S(1)} %copy-done.2, bf16[2,192,1024]{2,1,0:T(8,128)(2,1)} %get-tuple-element.20.own, ...), custom_call_target="tpu_custom_call", output_to_operand_aliasing={{0}: (1, {})} | custom-call | flops 1610612736 | bytes 20971520 | tf_op jit(solution)/shard_map/ahead/pallas_call | solution.py:228
  201.6 1.6 copy-done.3
  203.2 7.8 %finish.6 = (bf16[2,192,1024]{2,1,0:T(8,128)(2,1)}, bf16[3,2,192,1024]{3,2,1,0:T(8,128)(2,1)S(1)}) custom-call(s32[5]{0:T(128)S(1)} %stack.191.info, f32[2,2,192,1024]{3,2,1,0:T(8,128)} %copy-done.3, bf16[2,192,1024]{2,1,0:T(8,128)(2,1)} %collective-permute-done.6.a, bf16[16,4,32,1024]{3,2,1,0:T(8,128)(2,1)} %bitcast.61, ...), custom_call_target="tpu_custom_call", output_to_operand_aliasing={{1}: (9, {})} | custom-call | flops 3221225472 | bytes 25165824 | tf_op jit(solution)/shard_map/finish/pallas_call | solution.py:201
  211.0 1.4 copy-done.6
  212.4 1.6 collective-permute-start.8
  214.0 0.1 stack.196.info
  214.1 0.1 pad_add_fusion.3
  214.2 1.3 collective-permute-start.10
  215.5 1.5 collective-permute-start.9
  217.0 7.0 %ahead.5 = (f32[2,2,192,1024]{3,2,1,0:T(8,128)}, bf16[2,192,1024]{2,1,0:T(8,128)(2,1)S(1)}) custom-call(s32[4]{0:T(128)S(1)} %get-tuple-element.43.info, f32[2,2,192,1024]{3,2,1,0:T(8,128)} %copy-done.3, bf16[2,192,1024]{2,1,0:T(8,128)(2,1)} %get-tuple-element.23.own, ...), custom_call_target="tpu_custom_call", output_to_operand_aliasing={{0}: (1, {})} | custom-call | flops 1610612736 | bytes 20971520 | tf_op jit(solution)/shard_map/ahead/pallas_call | solution.py:228
  223.9 0.9 copy-done.13
  224.9 7.7 %finish.7 = (bf16[2,192,1024]{2,1,0:T(8,128)(2,1)}, bf16[3,2,192,1024]{3,2,1,0:T(8,128)(2,1)S(1)}) custom-call(s32[5]{0:T(128)S(1)} %stack.196.info, f32[2,2,192,1024]{3,2,1,0:T(8,128)} %get-tuple-element.24.r, bf16[2,192,1024]{2,1,0:T(8,128)(2,1)} %collective-permute-done.8.a, bf16[16,4,32,1024]{3,2,1,0:T(8,128)(2,1)} %bitcast.62, ...), custom_call_target="tpu_custom_call", output_to_operand_aliasing={{1}: (9, {})} | custom-call | flops 3221225472 | bytes 25165824 | tf_op jit(solution)/shard_map/finish/pallas_call | solution.py:201
  232.6 1.4 copy-done.8
  234.1 1.3 collective-permute-start.11
  235.4 0.1 stack.201.info
  235.4 1.3 collective-permute-start.13
  236.7 1.3 collective-permute-start.12
  238.0 26.3 %collective-permute-done.10.c = bf16[2,192,1024]{2,1,0:T(8,128)(2,1)} collective-permute-done((bf16[2,192,1024]{2,1,0:T(8,128)(2,1)}, bf16[2,192,1024]{2,1,0:T(8,128)(2,1)}, u32[]{:S(2)}, u32[]{:S(2)}) %collective-permute-start.10) | collective-permute-done | bytes 786464 | tf_op jit(solution)/shard_map/ppermute | solution.py:142
  264.4 8.8 %ahead.6 = (f32[2,2,192,1024]{3,2,1,0:T(8,128)}, bf16[2,192,1024]{2,1,0:T(8,128)(2,1)}) custom-call(s32[4]{0:T(128)S(1)} %get-tuple-element.44.info, f32[2,2,192,1024]{3,2,1,0:T(8,128)} %get-tuple-element.24.r, bf16[2,192,1024]{2,1,0:T(8,128)(2,1)} %get-tuple-element.26.own, ...), custom_call_target="tpu_custom_call", output_to_operand_aliasing={{0}: (1, {})} | custom-call | flops 1610612736 | bytes 20971520 | tf_op jit(solution)/shard_map/ahead/pallas_call | solution.py:228
  273.1 5.2 %collective-permute-done.11.a = bf16[2,192,1024]{2,1,0:T(8,128)(2,1)S(1)} collective-permute-done((bf16[2,192,1024]{2,1,0:T(8,128)(2,1)}, bf16[2,192,1024]{2,1,0:T(8,128)(2,1)S(1)}, u32[]{:S(2)}, u32[]{:S(2)}) %collective-permute-start.11) | collective-permute-done | bytes 786464 | tf_op jit(solution)/shard_map/ppermute | solution.py:142
  278.3 10.5 %finish.8 = (bf16[2,192,1024]{2,1,0:T(8,128)(2,1)}, bf16[3,2,192,1024]{3,2,1,0:T(8,128)(2,1)S(1)}) custom-call(s32[5]{0:T(128)S(1)} %stack.201.info, f32[2,2,192,1024]{3,2,1,0:T(8,128)} %get-tuple-element.28.r, bf16[2,192,1024]{2,1,0:T(8,128)(2,1)S(1)} %collective-permute-done.11.a, ...), custom_call_target="tpu_custom_call", output_to_operand_aliasing={{1}: (9, {})} | custom-call | flops 3221225472 | bytes 25165824 | tf_op jit(solution)/shard_map/finish/pallas_call | solution.py:201
  288.8 1.4 copy-done.10
  290.2 1.5 collective-permute-start.14
  291.8 0.1 stack.162.info
  291.9 6.2 %collective-permute-done.13.c = bf16[2,192,1024]{2,1,0:T(8,128)(2,1)} collective-permute-done((bf16[2,192,1024]{2,1,0:T(8,128)(2,1)}, bf16[2,192,1024]{2,1,0:T(8,128)(2,1)}, u32[]{:S(2)}, u32[]{:S(2)}) %collective-permute-start.13) | collective-permute-done | bytes 786464 | tf_op jit(solution)/shard_map/ppermute | solution.py:142
  298.1 8.7 %ahead.7 = (f32[2,2,192,1024]{3,2,1,0:T(8,128)}, bf16[2,192,1024]{2,1,0:T(8,128)(2,1)}) custom-call(s32[4]{0:T(128)S(1)} %get-tuple-element.45.info, f32[2,2,192,1024]{3,2,1,0:T(8,128)} %get-tuple-element.28.r, bf16[2,192,1024]{2,1,0:T(8,128)(2,1)} %get-tuple-element.30.own, ...), custom_call_target="tpu_custom_call", output_to_operand_aliasing={{0}: (1, {})} | custom-call | flops 1610612736 | bytes 20971520 | tf_op jit(solution)/shard_map/ahead/pallas_call | solution.py:228
  306.8 2.5 collective-permute-done.14.a
  309.3 10.4 %finish.9 = (bf16[2,192,1024]{2,1,0:T(8,128)(2,1)}, bf16[3,2,192,1024]{3,2,1,0:T(8,128)(2,1)S(1)}) custom-call(s32[5]{0:T(128)S(1)} %stack.162.info, f32[2,2,192,1024]{3,2,1,0:T(8,128)} %get-tuple-element.32.r, bf16[2,192,1024]{2,1,0:T(8,128)(2,1)S(1)} %collective-permute-done.14.a, ...), custom_call_target="tpu_custom_call", output_to_operand_aliasing={{1}: (9, {})} | custom-call | flops 3221225472 | bytes 25165824 | tf_op jit(solution)/shard_map/finish/pallas_call | solution.py:201
  319.7 0.1 slice.23
  319.9 0.2 constant_dynamic-slice_fusion.1
  320.1 3.1 collective-permute-start.15
  323.1 1.9 collective-permute-done.15
  325.1 1.8 maximum_select_fusion
  (38 shorter events, 0.3 us)
Async XLA Ops:
  6.5 168.6 %copy-start = (bf16[768,1024]{1,0:T(8,128)(2,1)S(1)}, bf16[768,1024]{1,0:T(8,128)(2,1)}, u32[]{:S(2)}) copy-start(bf16[768,1024]{1,0:T(8,128)(2,1)} %param.4) | copy-start | bytes 4718596
  6.5 59.5 %all-gather.7.cloned.1.call-start = ((), (), s32[]{:S(2)}) async-start(), calls=%async_computation | async-start | bytes 4456448 | tf_op jit(solution)/shard_map/all_gather | solution.py:158
  8.4 3.4 %collective-permute-start = (bf16[32,512]{1,0:T(8,128)(2,1)S(1)}, bf16[32,512]{1,0:T(8,128)(2,1)S(1)}, u32[]{:S(2)}, u32[]{:S(2)}) collective-permute-start(bf16[32,512]{1,0:T(8,128)(2,1)S(1)} %get-tuple-element.42), channel_id=1, source_target_pairs={{1,0},{3,2},{5,4},{7,6},{9,8},{11,10},{13,12},{15,14},{17,16},{19,... | collective-permute-start | bytes 98312 | tf_op jit(solution)/shard_map/ppermute | solution.py:152
  13.5 105.8 %all-gather.9.cloned.1.call-start = ((), (), s32[]{:S(2)}) async-start(), calls=%async_computation.1 | async-start | bytes 4456448 | tf_op jit(solution)/shard_map/all_gather | solution.py:158
  14.3 158.3 %all-gather.11.cloned.1.call-start = ((), (), s32[]{:S(2)}) async-start(), calls=%async_computation.2 | async-start | bytes 4456448 | tf_op jit(solution)/shard_map/all_gather | solution.py:158
  15.3 6.9 %collective-permute-start.4 = (bf16[4,32,1024]{2,1,0:T(8,128)(2,1)S(1)}, bf16[4,32,1024]{2,1,0:T(8,128)(2,1)S(1)}, u32[]{:S(2)}, u32[]{:S(2)}) collective-permute-start(bf16[4,32,1024]{2,1,0:T(8,128)(2,1)S(1)} %slice.28), channel_id=1, source_target_pairs={{6,0},{7,1},{14,8},{15,9},{22,16},{23,17},{30,24},{31,25},{38,32},... | collective-permute-start | bytes 786440 | tf_op jit(solution)/shard_map/ppermute | solution.py:142
  66.1 109.1 %collective-permute-start.1 = (bf16[16,128,1024]{2,1,0:T(8,128)(2,1)}, bf16[16,128,1024]{2,1,0:T(8,128)(2,1)}, u32[]{:S(2)}, u32[]{:S(2)}) collective-permute-start(bf16[16,128,1024]{2,1,0:T(8,128)(2,1)} %bitcast.52), channel_id=1, source_target_pairs={{0,1},{1,0},{2,3},{3,2},{4,5},{5,4},{6,7},{7,6},{8,9},{9,8},{10,11... | collective-permute-start | bytes 12582920 | tf_op jit(solution)/shard_map/ppermute | solution.py:145
  119.3 62.4 %collective-permute-start.2 = (bf16[16,4,32,1024]{3,2,1,0:T(8,128)(2,1)}, bf16[16,4,32,1024]{3,2,1,0:T(8,128)(2,1)}, u32[]{:S(2)}, u32[]{:S(2)}) collective-permute-start(bf16[16,4,32,1024]{3,2,1,0:T(8,128)(2,1)} %bitcast.59), channel_id=1, source_target_pairs={{0,1},{1,0},{2,3},{3,2},{4,5},{5,4},{6,7},{7,6},{8,9},{9,8},{10,11... | collective-permute-start | bytes 12582920 | tf_op jit(solution)/shard_map/ppermute | solution.py:145
  172.6 21.8 %collective-permute-start.5 = (bf16[16,4,32,1024]{3,2,1,0:T(8,128)(2,1)}, bf16[16,4,32,1024]{3,2,1,0:T(8,128)(2,1)}, u32[]{:S(2)}, u32[]{:S(2)}) collective-permute-start(bf16[16,4,32,1024]{3,2,1,0:T(8,128)(2,1)} %bitcast.65), channel_id=1, source_target_pairs={{0,1},{1,0},{2,3},{3,2},{4,5},{5,4},{6,7},{7,6},{8,9},{9,8},{10,11... | collective-permute-start | bytes 12582920 | tf_op jit(solution)/shard_map/ppermute | solution.py:145
  174.8 6.9 %collective-permute-start.3 = (bf16[2,512,512]{2,1,0:T(8,128)(2,1)S(1)}, bf16[2,512,512]{2,1,0:T(8,128)(2,1)}, u32[]{:S(2)}, u32[]{:S(2)}) collective-permute-start(bf16[2,512,512]{2,1,0:T(8,128)(2,1)S(1)} %bitcast.46), channel_id=1, source_target_pairs={{0,1},{1,0},{2,3},{3,2},{4,5},{5,4},{6,7},{7,6},{8,9},{9,8},{10,11... | collective-permute-start | bytes 3145736 | tf_op jit(solution)/shard_map/ppermute | solution.py:145
  180.0 1.6 copy-start.1
  189.7 1.5 copy-start.4
  191.1 12.1 %collective-permute-start.6 = (bf16[2,192,1024]{2,1,0:T(8,128)(2,1)}, bf16[2,192,1024]{2,1,0:T(8,128)(2,1)}, u32[]{:S(2)}, u32[]{:S(2)}) collective-permute-start(bf16[2,192,1024]{2,1,0:T(8,128)(2,1)} %get-tuple-element.20.own), channel_id=1, source_target_pairs={{0,2},{1,3},{8,10},{9,11},{16,18},{17,19},{24,26},{25,27},{32,34},... | collective-permute-start | bytes 2359304 | tf_op jit(solution)/shard_map/ppermute | solution.py:142
  192.9 24.1 %collective-permute-start.7 = (bf16[2,192,1024]{2,1,0:T(8,128)(2,1)}, bf16[2,192,1024]{2,1,0:T(8,128)(2,1)}, u32[]{:S(2)}, u32[]{:S(2)}) collective-permute-start(bf16[2,192,1024]{2,1,0:T(8,128)(2,1)} %get-tuple-element.20.own), channel_id=1, source_target_pairs={{0,4},{1,5},{8,12},{9,13},{16,20},{17,21},{24,28},{25,29},{32,36},... | collective-permute-start | bytes 2359304 | tf_op jit(solution)/shard_map/ppermute | solution.py:142
  194.5 1.9 copy-start.2
  196.4 6.8 %copy-start.5 = (bf16[3,2,192,1024]{3,2,1,0:T(8,128)(2,1)S(1)}, bf16[3,2,192,1024]{3,2,1,0:T(8,128)(2,1)}, u32[]{:S(2)}) copy-start(bf16[3,2,192,1024]{3,2,1,0:T(8,128)(2,1)} %copy-done.4) | copy-start | bytes 7077892
  201.6 1.6 copy-start.3
  203.2 7.8 %copy-start.12 = (bf16[2,192,1024]{2,1,0:T(8,128)(2,1)}, bf16[2,192,1024]{2,1,0:T(8,128)(2,1)S(1)}, u32[]{:S(2)}) copy-start(bf16[2,192,1024]{2,1,0:T(8,128)(2,1)S(1)} %get-tuple-element.27) | copy-start | bytes 2359300
  211.0 1.5 copy-start.6
  212.4 12.4 %collective-permute-start.8 = (bf16[2,192,1024]{2,1,0:T(8,128)(2,1)}, bf16[2,192,1024]{2,1,0:T(8,128)(2,1)}, u32[]{:S(2)}, u32[]{:S(2)}) collective-permute-start(bf16[2,192,1024]{2,1,0:T(8,128)(2,1)} %get-tuple-element.23.own), channel_id=1, source_target_pairs={{0,2},{1,3},{2,4},{3,5},{8,10},{9,11},{10,12},{11,13},{16,18},{17,... | collective-permute-start | bytes 2359304 | tf_op jit(solution)/shard_map/ppermute | solution.py:142
  214.2 50.2 %collective-permute-start.10 = (bf16[2,192,1024]{2,1,0:T(8,128)(2,1)}, bf16[2,192,1024]{2,1,0:T(8,128)(2,1)}, u32[]{:S(2)}, u32[]{:S(2)}) collective-permute-start(bf16[2,192,1024]{2,1,0:T(8,128)(2,1)} %copy-done.12), channel_id=1, source_target_pairs={{0,6},{1,7},{8,14},{9,15},{16,22},{17,23},{24,30},{25,31},{32,38},... | collective-permute-start | bytes 2359304 | tf_op jit(solution)/shard_map/ppermute | solution.py:142
  215.5 48.9 %collective-permute-start.9 = (bf16[2,192,1024]{2,1,0:T(8,128)(2,1)}, bf16[2,192,1024]{2,1,0:T(8,128)(2,1)}, u32[]{:S(2)}, u32[]{:S(2)}) collective-permute-start(bf16[2,192,1024]{2,1,0:T(8,128)(2,1)} %get-tuple-element.23.own), channel_id=1, source_target_pairs={{0,4},{1,5},{2,6},{3,7},{8,12},{9,13},{10,14},{11,15},{16,20},{17,... | collective-permute-start | bytes 2359304 | tf_op jit(solution)/shard_map/ppermute | solution.py:142
  217.0 7.9 %copy-start.7 = (bf16[3,2,192,1024]{3,2,1,0:T(8,128)(2,1)S(1)}, bf16[3,2,192,1024]{3,2,1,0:T(8,128)(2,1)}, u32[]{:S(2)}) copy-start(bf16[3,2,192,1024]{3,2,1,0:T(8,128)(2,1)} %copy-done.6) | copy-start | bytes 7077892
  223.9 0.9 copy-start.13
  232.6 1.5 copy-start.8
  234.1 44.3 %collective-permute-start.11 = (bf16[2,192,1024]{2,1,0:T(8,128)(2,1)}, bf16[2,192,1024]{2,1,0:T(8,128)(2,1)S(1)}, u32[]{:S(2)}, u32[]{:S(2)}) collective-permute-start(bf16[2,192,1024]{2,1,0:T(8,128)(2,1)} %get-tuple-element.26.own), channel_id=1, source_target_pairs={{2,4},{3,5},{4,6},{5,7},{10,12},{11,13},{12,14},{13,15},{18,20},{1... | collective-permute-start | bytes 2359304 | tf_op jit(solution)/shard_map/ppermute | solution.py:142
  235.4 62.6 %collective-permute-start.13 = (bf16[2,192,1024]{2,1,0:T(8,128)(2,1)}, bf16[2,192,1024]{2,1,0:T(8,128)(2,1)}, u32[]{:S(2)}, u32[]{:S(2)}) collective-permute-start(bf16[2,192,1024]{2,1,0:T(8,128)(2,1)} %copy-done.13), channel_id=1, source_target_pairs={{0,6},{1,7},{8,14},{9,15},{16,22},{17,23},{24,30},{25,31},{32,38},... | collective-permute-start | bytes 2359304 | tf_op jit(solution)/shard_map/ppermute | solution.py:142
  236.7 61.3 %collective-permute-start.12 = (bf16[2,192,1024]{2,1,0:T(8,128)(2,1)}, bf16[2,192,1024]{2,1,0:T(8,128)(2,1)}, u32[]{:S(2)}, u32[]{:S(2)}) collective-permute-start(bf16[2,192,1024]{2,1,0:T(8,128)(2,1)} %get-tuple-element.26.own), channel_id=1, source_target_pairs={{2,6},{3,7},{10,14},{11,15},{18,22},{19,23},{26,30},{27,31},{34,38... | collective-permute-start | bytes 2359304 | tf_op jit(solution)/shard_map/ppermute | solution.py:142
  264.4 14.0 %copy-start.9 = (bf16[3,2,192,1024]{3,2,1,0:T(8,128)(2,1)S(1)}, bf16[3,2,192,1024]{3,2,1,0:T(8,128)(2,1)}, u32[]{:S(2)}) copy-start(bf16[3,2,192,1024]{3,2,1,0:T(8,128)(2,1)} %copy-done.8) | copy-start | bytes 7077892
  288.8 1.5 copy-start.10
  290.2 19.0 %collective-permute-start.14 = (bf16[2,192,1024]{2,1,0:T(8,128)(2,1)}, bf16[2,192,1024]{2,1,0:T(8,128)(2,1)S(1)}, u32[]{:S(2)}, u32[]{:S(2)}) collective-permute-start(bf16[2,192,1024]{2,1,0:T(8,128)(2,1)} %get-tuple-element.30.own), channel_id=1, source_target_pairs={{4,6},{5,7},{12,14},{13,15},{20,22},{21,23},{28,30},{29,31},{36,38... | collective-permute-start | bytes 2359304 | tf_op jit(solution)/shard_map/ppermute | solution.py:142
  298.1 11.2 %copy-start.11 = (bf16[3,2,192,1024]{3,2,1,0:T(8,128)(2,1)S(1)}, bf16[3,2,192,1024]{3,2,1,0:T(8,128)(2,1)}, u32[]{:S(2)}) copy-start(bf16[3,2,192,1024]{3,2,1,0:T(8,128)(2,1)} %copy-done.10) | copy-start | bytes 7077892
  320.1 5.0 %collective-permute-start.15 = (bf16[384,1024]{1,0:T(8,128)(2,1)S(1)}, bf16[384,1024]{1,0:T(8,128)(2,1)S(1)}, u32[]{:S(2)}, u32[]{:S(2)}) collective-permute-start(bf16[384,1024]{1,0:T(8,128)(2,1)S(1)} %bitcast.72), channel_id=1, source_target_pairs={{0,1},{1,0},{2,3},{3,2},{4,5},{5,4},{6,7},{7,6},{8,9},{9,8},{10,11... | collective-permute-start | bytes 2359304 | tf_op jit(solution)/shard_map/ppermute | solution.py:145
Sparse Core Ops, SparseCore 0:
  13.7 52.3 all-gather.6
  68.2 51.1 all-gather.8
  121.5 51.1 all-gather.10

commit v2 on v0

v2 whole, which is shorter than its diff:
```python
import functools
import math

import jax
import jax.numpy as jnp
from jax import lax
from jax.experimental import pallas as pl
from jax.experimental.pallas import tpu as pltpu
from jax.sharding import PartitionSpec as P

CHUNKS = 2
SIDE = 4
BF = jnp.bfloat16
F32 = jnp.float32
ANY = pl.BlockSpec(memory_space=pl.ANY)
SMEM = pl.BlockSpec(memory_space=pltpu.SMEM)
VMEM = pl.BlockSpec(memory_space=pltpu.VMEM)


def mm(a, b):
    return jnp.dot(a, b, preferred_element_type=F32)


def after(x, *deps):
    return lax.optimization_barrier((x, *deps))[0]


PIECES = ((0, (0, 1, 2, 3)), (1, (0, 1, 2, 3)), (3, (0, 1, 2, 3)), (2, (0, 1)), (2, (2, 3)))
N_PIECES = 2 * len(PIECES)


def piece_places(info):
    core, y, x = info[1], info[2], info[3]
    for which, parity in ((0, core), (1, 1 - core)):
        for i, (e, along) in enumerate(PIECES):
            for j, d in enumerate(along):
                dy, dx = jnp.where(parity == 0, e, d), jnp.where(parity == 0, d, e)
                yield which * len(PIECES) + i, j, parity, ((y + dy) % SIDE) * SIDE + (x + dx) % SIDE


def start_diag(info, head, dt_own, dt_oth, gv, dv, sem):
    core = info[1]
    depth = gv.shape[2]
    pltpu.make_async_copy(head.at[:, :, pl.ds(head.shape[2] - depth, depth)], gv, sem.at[0]).start()
    pltpu.make_async_copy(dt_own, dv.at[core], sem.at[1]).start()
    pltpu.make_async_copy(dt_oth, dv.at[1 - core], sem.at[1]).start()


def wait_diag(gv, dv, sem):
    pltpu.make_async_copy(gv, gv, sem.at[0]).wait()
    pltpu.make_async_copy(dv, dv, sem.at[1]).wait()


def solve(running, diag, dt, f):
    size = dt.shape[-1]

    def column(i):
        return running[i // 2, :, (i % 2) * size:(i % 2 + 1) * size]

    def store(i, value):
        f[i // 2, :, (i % 2) * size:(i % 2 + 1) * size] = value

    def left(i, k):
        slab = diag.shape[2] // 3
        block = diag[i // 2, :, k * slab:(k + 1) * slab, (i % 2) * size:(i % 2 + 1) * size]
        return block.reshape(size, size)

    f0 = mm(column(0).astype(BF), dt[0, 0]).astype(BF)
    store(0, f0)
    f1 = mm((column(1) - mm(f0, left(1, 0))).astype(BF), dt[0, 1]).astype(BF)
    store(1, f1)
    f2 = mm((column(2) - mm(f0, left(2, 0)) - mm(f1, left(2, 1))).astype(BF), dt[1, 0]).astype(BF)
    store(2, f2)
    f3 = column(3) - mm(f0, left(3, 0)) - mm(f1, left(3, 1)) - mm(f2, left(3, 2))
    store(3, mm(f3.astype(BF), dt[1, 1]).astype(BF))


def pick_kernel(info, first, other, out):
    out[...] = jnp.where(info[0] == 1, first[...], other[...])


def scores_kernel(scale, info, emb, dt_own, dt_oth, head, *refs):
    out, f, (lm, gv, dv, sem) = refs[:CHUNKS], refs[CHUNKS:2 * CHUNKS], refs[2 * CHUNKS:]
    plane = info[0]
    lead = lm.shape[2]
    t = out[0].shape[1]
    copies = [pltpu.make_async_copy(head.at[i, :, pl.ds(0, lead)], lm.at[i], sem.at[2 + i]) for i in range(2)]
    for copy in copies:
        copy.start()
    pl.when(plane == 0)(lambda: start_diag(info, head, dt_own, dt_oth, gv, dv, sem))
    for half in range(2):
        copies[half].wait()
        points = lm[half].reshape(emb.shape[1], lm.shape[3])
        for q in range(CHUNKS):
            out[q][half] = jnp.exp(mm(emb[q * t:(q + 1) * t, :], points) * scale)

    @pl.when(plane == 0)
    def _():
        wait_diag(gv, dv, sem)
        for q in range(CHUNKS):
            solve(out[q], gv, dv, f[q])


def start_factor(factor, lv, sems):
    copies = []
    for half in range(2):
        copies.append(pltpu.make_async_copy(factor.at[half], lv.at[half], sems.at[half]))
        copies[-1].start()
    return copies


def subtract(acc, av, lv, copies):
    size = lv.shape[1] * lv.shape[3]
    for half in range(2):
        copies[half].wait()
        for k in range(lv.shape[2]):
            left = av[k // 2, :, (k % 2) * size:(k % 2 + 1) * size]
            acc[half] -= mm(left, lv[half, :, k].reshape(size, -1))


def finish_kernel(role, q, info, r, a, head, dt_own, dt_oth, *refs):
    last = role == SIDE - 1
    pieces, refs = refs[:N_PIECES], refs[N_PIECES:]
    if last:
        part, earlier, refs = refs[0], refs[1:SIDE], refs[SIDE:]
        keep, give, f, pv, acc, av, lv, gv, dv, sems, sem = refs
    else:
        f, acc, av, lv, gv, dv, sems, sem = refs
    plane, core = info[0], info[1]
    t = acc.shape[1]

    @pl.when(plane == role)
    def _():
        ca = pltpu.make_async_copy(a, av, sems.at[2])
        cr = pltpu.make_async_copy(r, acc, sems.at[3])
        ca.start()
        cr.start()
        for i, d, parity, place in piece_places(info):
            pltpu.make_async_copy(pieces[i].at[d], lv.at[parity, place], sems.at[parity]).start()
        start_diag(info, head, dt_own, dt_oth, gv, dv, sem)
        if last:
            cp = pltpu.make_async_copy(part.at[:, pl.ds(q * t, t)], pv, sems.at[6])
            cp.start()
        ca.wait()
        cr.wait()
        if last:
            cp.wait()
            acc[...] += pv[...].astype(F32)
        subtract(acc, av, lv, [pltpu.make_async_copy(lv.at[half], lv.at[half], sems.at[half]) for half in range(2)])
        wait_diag(gv, dv, sem)
        solve(acc, gv, dv, f)
        if last:
            keep[...] = f[pl.ds(core, 1)][0]
            give[...] = f[pl.ds(1 - core, 1)][0]

    if last:
        for z, done in enumerate(earlier):

            @pl.when(plane == z)
            def _():
                c0 = pltpu.make_async_copy(done.at[core], keep, sems.at[0])
                c1 = pltpu.make_async_copy(done.at[1 - core], give, sems.at[1])
                c0.start()
                c1.start()
                c0.wait()
                c1.wait()


def partial_kernel(info, factor, *refs):
    own, (p, acc, av, lv, sems) = refs[:CHUNKS], refs[CHUNKS:]
    t = own[0].shape[1]

    @pl.when(info[0] == 1)
    def _():
        moves = [pltpu.make_async_copy(own[q], av.at[:, pl.ds(q * t, t)], sems.at[2 + q]) for q in range(CHUNKS)]
        for move in moves:
            move.start()
        copies = start_factor(factor, lv, sems)
        acc[...] = jnp.zeros_like(acc)
        for move in moves:
            move.wait()
        subtract(acc, av, lv, copies)
        p[...] = acc[...].astype(BF)


def update_kernel(info, factor, r, to_3, to_2, r_out, acc, av, lv, sems):
    @pl.when(info[0] >= 2)
    def _():
        copies = start_factor(factor, lv, sems)
        cr = pltpu.make_async_copy(r, acc, sems.at[2])
        cr.start()
        for plane, a in ((2, to_2), (3, to_3)):
            pl.when(info[0] == plane)(lambda a=a: pltpu.make_async_copy(a, av, sems.at[3]).start())
        cr.wait()
        pltpu.make_async_copy(to_2, av, sems.at[3]).wait()
        subtract(acc, av, lv, copies)
        out = pltpu.make_async_copy(acc, r_out, sems.at[2])
        out.start()
        out.wait()


def params(mib=60):
    return pltpu.CompilerParams(vmem_limit_bytes=mib << 20)


def cost(us):
    return pl.CostEstimate(flops=us * 1_000_000_000, bytes_accessed=1 << 10, transcendentals=0)


def per_device(embeddings, landmarks, factor_rows, diag_inverse):
    tokens, depth = embeddings.shape
    rows = lax.axis_size("rows")
    planes = lax.axis_size("cols") // 2
    here = lax.axis_index("cols")
    plane, core = here // 2, here % 2
    row = lax.axis_index("rows")
    own_rows, blocks, slab = factor_rows.shape
    size = diag_inverse.shape[1]
    lead = landmarks.shape[1]
    n = CHUNKS
    half = tokens // 2
    t = half // n
    scale = 0.5 / math.sqrt(depth)
    per_plane = blocks // planes
    info = jnp.stack([plane, core, row // SIDE, row % SIDE]).astype(jnp.int32)

    def send(x, source, target):
        return lax.ppermute(x, "cols", [(2 * source + k, 2 * target + k) for k in range(2)])

    def swap(x):
        return lax.ppermute(x, "cols", [(c, c ^ 1) for c in range(2 * planes)])

    def fetch(x, by, second):
        pairs = []
        for y in range(SIDE):
            for q in range(SIDE):
                for c in range(2, 2 * planes):
                    along_x = (c % 2 == 0) != second
                    sy, sx = (y, (q + by) % SIDE) if along_x else ((y + by) % SIDE, q)
                    pairs.append(((sy * SIDE + sx) * 2 * planes + c, (y * SIDE + q) * 2 * planes + c))
        return lax.ppermute(x, ("rows", "cols"), pairs)

    def line_of(x):
        return jnp.stack([x] + [fetch(x, by, False) for by in range(1, SIDE)])

    def spread(line):
        up, down = fetch(line, 1, True), fetch(line, 3, True)
        mid = SIDE // 2
        return [line, up, down, fetch(up[:mid], 1, True), fetch(down[mid:], 3, True)]

    ft = factor_rows.transpose(1, 2, 0)
    groups = [[r * 2 * planes + 2 * z + k for k in range(2) for r in range(rows)] for z in range(planes)]

    def gather(x):
        everyone = lax.all_gather(x, ("rows", "cols"), axis=0, axis_index_groups=groups)
        return everyone.reshape(2, rows, *x.shape)

    diag = lax.dynamic_slice_in_dim(ft, per_plane * plane, per_plane - 1, 0)
    head = gather(jnp.concatenate([landmarks.T, diag.reshape(-1, own_rows)], axis=0))
    dt_own = diag_inverse.transpose(0, 2, 1)
    dt_oth = swap(dt_own)

    late = line_of(lax.dynamic_slice_in_dim(ft, per_plane * jnp.maximum(plane - 1, 0), per_plane, 0))
    late = spread(late)

    first = send(after(ft[per_plane:2 * per_plane], *late[1:3]), 3, 1)
    factor = gather(
        pl.pallas_call(
            pick_kernel,
            in_specs=[SMEM, VMEM, VMEM],
            out_specs=VMEM,
            out_shape=jax.ShapeDtypeStruct(first.shape, BF),
            cost_estimate=cost(60),
            name="pick",
        )(info, first, ft[:per_plane])
    )

    emb = lax.dynamic_slice_in_dim(embeddings, core * half, half, 0)
    chunk_f32 = jax.ShapeDtypeStruct((2, t, own_rows), F32)
    chunk_bf = jax.ShapeDtypeStruct((2, t, own_rows), BF)
    whole_bf = jax.ShapeDtypeStruct((2, half, own_rows), BF)
    diag_scratch = [
        pltpu.VMEM((2, rows, (per_plane - 1) * slab, own_rows), BF),
        pltpu.VMEM((2, 2, size, size), BF),
    ]
    factor_scratch = [
        pltpu.VMEM(whole_bf.shape, F32),
        pltpu.VMEM(whole_bf.shape, BF),
        pltpu.VMEM((2, rows, per_plane, slab, own_rows), BF),
        pltpu.SemaphoreType.DMA((7,)),
    ]
    out = pl.pallas_call(
        functools.partial(scores_kernel, scale),
        in_specs=[SMEM, VMEM] + [ANY] * 3,
        out_specs=[VMEM] * (2 * n),
        out_shape=[chunk_f32] * n + [chunk_bf] * n,
        scratch_shapes=[pltpu.VMEM((2, rows, lead, own_rows), BF)] + diag_scratch + [pltpu.SemaphoreType.DMA((4,))],
        compiler_params=params(),
        cost_estimate=cost(3),
        name="scores",
    )(info, after(emb, *late[:3]), dt_own, dt_oth, head)
    r, f0 = out[:n], out[n:]
    f0_to_1 = [send(x, 0, 1) for x in f0]
    f0_to_3 = [send(x, 0, 3) for x in f0]
    f0_to_2 = [send(x, 3, 2) for x in f0_to_3]
    late = late + [swap(x) for x in late]
    factor = after(factor, f0[-1])

    def finish(role, q, r, a, more=()):
        last = role == planes - 1
        one = jax.ShapeDtypeStruct((t, own_rows), BF)
        return pl.pallas_call(
            functools.partial(finish_kernel, role, q),
            in_specs=[SMEM] + [ANY] * (5 + N_PIECES + len(more)),
            out_specs=[VMEM] * 2 if last else VMEM,
            out_shape=[one, one] if last else chunk_bf,
            scratch_shapes=([pltpu.VMEM(chunk_bf.shape, BF)] * 2 if last else [])
            + [pltpu.VMEM(chunk_f32.shape, F32), pltpu.VMEM(chunk_bf.shape, BF), factor_scratch[2]]
            + diag_scratch
            + [factor_scratch[3], pltpu.SemaphoreType.DMA((2,))],
            compiler_params=params(),
            cost_estimate=cost(3),
            name=f"finish{role}",
        )(info, r, a, head, dt_own, dt_oth, *late, *more)

    def partial(own):
        return pl.pallas_call(
            partial_kernel,
            in_specs=[SMEM] + [ANY] * (1 + n),
            out_specs=VMEM,
            out_shape=whole_bf,
            scratch_shapes=factor_scratch,
            compiler_params=params(),
            cost_estimate=cost(0),
            name="partial",
        )(info, factor, *own)

    def update(r, to_3, to_2):
        return pl.pallas_call(
            update_kernel,
            in_specs=[SMEM] + [ANY] * 4,
            out_specs=ANY,
            out_shape=chunk_f32,
            scratch_shapes=[
                pltpu.VMEM(chunk_f32.shape, F32),
                pltpu.VMEM(chunk_bf.shape, BF),
            ]
            + factor_scratch[2:],
            compiler_params=params(),
            cost_estimate=cost(0),
            name="update",
        )(info, factor, r, to_3, to_2)

    f1 = []
    for q in range(n):
        f1.append(finish(1, q, r[q], after(f0_to_1[q], *f1)))
    f1_to_2 = [send(x, 1, 2) for x in f1]
    part = send(partial(f1), 1, 3)
    r2, f2 = [], []
    for q in range(n):
        r2.append(update(r[q], f0_to_3[q], after(f0_to_2[q], f1[-1], *f2)))
        f2.append(finish(2, q, r2[q], f1_to_2[q]))
    f2_to_3 = [send(x, 2, 3) for x in f2]
    done = []
    for q in range(n):
        a = after(f2_to_3[q], *[x[0] for x in done])
        done.append(finish(3, q, r2[q], a, (part, f0[q], f1[q], f2[q])))
    keep = [x for x, _ in done]
    got = [swap(x) for _, x in done]
    return jnp.where(core == 0, jnp.concatenate(keep + got, axis=0), jnp.concatenate(got + keep, axis=0))


def solution(mesh):
    in_specs = (P("rows", None), P("cols", "rows"), P("cols", None, "rows"), P("cols", None, None))
    out_specs = P("rows", "cols")
    return jax.shard_map(
        per_device, mesh=mesh, in_specs=in_specs, out_specs=out_specs, check_vma=False
    )
```

time: 894 us -> 241 us (0.27)
  waiting for transfers between devices: 651 us -> 94.8 us
  local copies, waits for them, and re-layouts: 167 us -> 10.9 us
  starting transfers between devices: 0.06 us -> 58.5 us
  Pallas kernels: 0 us -> 57.6 us
  matrix products: 48.3 us -> 0 us
    psum x7 -> x0, waiting for transfers between devices: 497 us -> none  [broadcast(): return lax.psum(jnp.where(mine, shard, jnp.zeros_like(shard)), axis)]
    all_gather x2, waiting for transfers between devices: 153 us -> 22.3 us  [gather(): lax.all_gather(x, ('rows', 'cols'), axis=0, axis_index_groups=groups)]
    dynamic_slice x14 -> x1, local copies, waits for them, and re-layouts: 109 us -> 0.94 us  [per_device(): emb = lax.dynamic_slice_in_dim(embeddings, core * half, half, 0)]
    ppermute x0 -> x27, waiting for transfers between devices: none -> 72.5 us  [the longest x12 37.3 us: send(): lax.ppermute(x, 'cols', [(2 * source + k, 2 * target + k) for k in range(...]
    ppermute x0 -> x27, starting transfers between devices: none -> 58.4 us  [the longest x7 21.2 us: fetch(): return lax.ppermute(x, ('rows', 'cols'), pairs)]
    pallas_call x0 -> x11, Pallas kernels: none -> 57.6 us  [the longest x6 30.7 us: finish(): pl.pallas_call(functools.partial(finish_kernel, role, q), in_specs=[SMEM]...]
    dot_general x10 -> x0, matrix products: 48.3 us -> none  [the longest x7 37.6 us: subtract_update(): lax.dot_general(arrived, flat, (((1,), (1,)), ((), ())), preferred_elemen...]
    cond x28 -> x0, local copies, waits for them, and re-layouts: 28.1 us -> none
  transfers between devices with their start and end apart: 9 -> 29, of which waited for: 9 -> 13; matrix products, arithmetic and copies ran while one was open for 1% -> 3% of each run, Pallas kernels for 0% -> 19%
where the time goes in v2:
time: 241 us
  waiting for transfers between devices  94.8 us (39%)
  starting transfers between devices  58.5 us (24%)
  Pallas kernels  57.6 us (24%)
  between operations  13.8 us (6%)
  local copies, waits for them, and re-layouts  10.9 us (5%)
  other arithmetic  5.03 us (2%)
    ppermute x12, waiting for transfers between devices, send(): lax.ppermute(x, 'cols', [(2 * source + k, 2 * target + k) for k in range(...  37.3 us
    ppermute x7, waiting for transfers between devices, fetch(): return lax.ppermute(x, ('rows', 'cols'), pairs)  33.2 us
    pallas_call x6, Pallas kernels, finish(): pl.pallas_call(functools.partial(finish_kernel, role, q), in_specs=[SMEM]...  30.7 us
    all_gather x2, waiting for transfers between devices, gather(): lax.all_gather(x, ('rows', 'cols'), axis=0, axis_index_groups=groups)  22.3 us
    ppermute x7, starting transfers between devices, fetch(): return lax.ppermute(x, ('rows', 'cols'), pairs)  21.2 us
    ppermute x12, starting transfers between devices, send(): lax.ppermute(x, 'cols', [(2 * source + k, 2 * target + k) for k in range(...  19.5 us
    ppermute x8, starting transfers between devices, swap(): return lax.ppermute(x, 'cols', [(c, c ^ 1) for c in range(2 * planes)])  17.7 us
    pallas_call x2, Pallas kernels, update(): pl.pallas_call(update_kernel, in_specs=[SMEM] + [ANY] * 4, out_specs=ANY,...  16.1 us
  transfers between devices with their start and end apart: 29, of which 13 were waited for; matrix products, arithmetic and copies ran while one was open for 3% of the time, Pallas kernels for 19%

profile of v2, /device:TPU:97, one launch (start us, length us, event | category | flops | bytes accessed | tf_op | source)
XLA Modules:
  0.0 240.7 jit_solution(8255231554937443690)
XLA Ops:
  6.5 1.1 constant_dynamic-slice_fusion
  7.6 1.7 pad_maximum_fusion.1
  9.4 4.6 %collective-permute-start = (bf16[4,32,1024]{2,1,0:T(8,128)(2,1)S(1)}, bf16[4,32,1024]{2,1,0:T(8,128)(2,1)S(1)}, u32[]{:S(2)}, u32[]{:S(2)}) collective-permute-start(bf16[4,32,1024]{2,1,0:T(8,128)(2,1)S(1)} %get-tuple-element.38), channel_id=1, source_target_pairs={{10,2},{35,3},{12,4},{37,5},{14,6},{39,7},{18,10},{43,11},{20,12},... | collective-permute-start | bytes 786440 | tf_op jit(solution)/shard_map/ppermute | solution.py:241
  14.1 2.3 collective-permute-start.1
  16.3 2.6 %collective-permute-start.2 = (bf16[4,32,1024]{2,1,0:T(8,128)(2,1)S(1)}, bf16[4,32,1024]{2,1,0:T(8,128)(2,1)S(1)}, u32[]{:S(2)}, u32[]{:S(2)}) collective-permute-start(bf16[4,32,1024]{2,1,0:T(8,128)(2,1)S(1)} %get-tuple-element.38), channel_id=1, source_target_pairs={{26,2},{99,3},{28,4},{101,5},{30,6},{103,7},{2,10},{107,11},{4,12}... | collective-permute-start | bytes 786440 | tf_op jit(solution)/shard_map/ppermute | solution.py:241
  19.0 4.0 %collective-permute-done.1 = bf16[4,32,1024]{2,1,0:T(8,128)(2,1)S(1)} collective-permute-done((bf16[4,32,1024]{2,1,0:T(8,128)(2,1)S(1)}, bf16[4,32,1024]{2,1,0:T(8,128)(2,1)S(1)}, u32[]{:S(2)}, u32[]{:S(2)}) %collective-permute-start.1) | collective-permute-done | bytes 262176 | tf_op jit(solution)/shard_map/ppermute | solution.py:241
  23.0 3.8 %collective-permute-done.2 = bf16[4,32,1024]{2,1,0:T(8,128)(2,1)S(1)} collective-permute-done((bf16[4,32,1024]{2,1,0:T(8,128)(2,1)S(1)}, bf16[4,32,1024]{2,1,0:T(8,128)(2,1)S(1)}, u32[]{:S(2)}, u32[]{:S(2)}) %collective-permute-start.2) | collective-permute-done | bytes 262176 | tf_op jit(solution)/shard_map/ppermute | solution.py:241
  26.8 0.1 pad_maximum_fusion.refs_0_
  26.9 4.5 %collective-permute-start.3 = (bf16[4,4,32,1024]{3,2,1,0:T(8,128)(2,1)S(1)}, bf16[4,4,32,1024]{3,2,1,0:T(8,128)(2,1)}, u32[]{:S(2)}, u32[]{:S(2)}) collective-permute-start(bf16[4,4,32,1024]{3,2,1,0:T(8,128)(2,1)S(1)} %pad_maximum_fusion.refs_0_), channel_id=1, source_target_pairs={{34,2},{11,3},{36,4},{13,5},{38,6},{15,7},{42,10},{19,11},{44,12},... | collective-permute-start | bytes 3145736 | tf_op jit(solution)/shard_map/ppermute | solution.py:241
  31.5 1.9 collective-permute-start.4
  33.4 0.8 fusion
  34.2 10.8 %collective-permute-done.3.refs_1_ = bf16[4,4,32,1024]{3,2,1,0:T(8,128)(2,1)} collective-permute-done((bf16[4,4,32,1024]{3,2,1,0:T(8,128)(2,1)S(1)}, bf16[4,4,32,1024]{3,2,1,0:T(8,128)(2,1)}, u32[]{:S(2)}, u32[]{:S(2)}) %collective-permute-start.3) | collective-permute-done | bytes 1048608 | tf_op jit(solution)/shard_map/ppermute | solution.py:241
  44.9 6.6 %collective-permute-done.4.refs_2_ = bf16[4,4,32,1024]{3,2,1,0:T(8,128)(2,1)} collective-permute-done((bf16[4,4,32,1024]{3,2,1,0:T(8,128)(2,1)S(1)}, bf16[4,4,32,1024]{3,2,1,0:T(8,128)(2,1)}, u32[]{:S(2)}, u32[]{:S(2)}) %collective-permute-start.4) | collective-permute-done | bytes 1048608 | tf_op jit(solution)/shard_map/ppermute | solution.py:241
  51.5 1.3 collective-permute-start.5
  52.8 0.6 pad_add_fusion.info
  53.4 2.7 %collective-permute-done.5.first = bf16[4,32,1024]{2,1,0:T(8,128)(2,1)S(1)} collective-permute-done((bf16[4,32,1024]{2,1,0:T(8,128)(2,1)S(1)}, bf16[4,32,1024]{2,1,0:T(8,128)(2,1)S(1)}, u32[]{:S(2)}, u32[]{:S(2)}) %collective-permute-start.5) | collective-permute-done | bytes 262176 | tf_op jit(solution)/shard_map/ppermute | solution.py:228
  56.1 0.7 copy-done.11
  56.8 1.8 pick.1
  58.6 1.5 copy.6
  60.1 15.2 %collective-permute-start.6 = (bf16[2,512,512]{2,1,0:T(8,128)(2,1)S(1)}, bf16[2,512,512]{2,1,0:T(8,128)(2,1)}, u32[]{:S(2)}, u32[]{:S(2)}) collective-permute-start(bf16[2,512,512]{2,1,0:T(8,128)(2,1)S(1)} %bitcast.30), channel_id=1, source_target_pairs={{0,1},{1,0},{2,3},{3,2},{4,5},{5,4},{6,7},{7,6},{8,9},{9,8},{10,11... | collective-permute-start | bytes 3145736 | tf_op jit(solution)/shard_map/ppermute | solution.py:231
  75.3 0.1 collective-permute-start.13
  75.4 0.9 constant_dynamic-slice_fusion.1.emb
  76.4 1.9 slice.18
  78.2 1.9 collective-permute-start.11
  80.2 0.5 collective-permute-start.14
  80.7 0.1 collective-permute-start.15
  80.8 7.0 %scores.1 = (f32[2,192,1024]{2,1,0:T(8,128)}, f32[2,192,1024]{2,1,0:T(8,128)}, bf16[2,192,1024]{2,1,0:T(8,128)(2,1)}, bf16[2,192,1024]{2,1,0:T(8,128)(2,1)}) custom-call(s32[4]{0:T(128)} %pad_add_fusion.info, bf16[384,1024]{1,0:T(8,128)(2,1)} %constant_dynamic-slice_fusion.1.emb, bf16[2,512,512]{2,1,0:T(8,128)(2,1)} %bitcast.31, ...), custom_call_target="tpu_custom_call" | custom-call | flops 3000000000 | bytes 1024 | tf_op jit(solution)/shard_map/scores/pallas_call | solution.py:292
  87.8 1.6 collective-permute-start.10
  89.4 1.1 slice.19
  90.5 3.4 %collective-permute-start.12 = (bf16[2,4,32,1024]{3,2,1,0:T(8,128)(2,1)S(1)}, bf16[2,4,32,1024]{3,2,1,0:T(8,128)(2,1)S(1)}, u32[]{:S(2)}, u32[]{:S(2)}) collective-permute-start(bf16[2,4,32,1024]{3,2,1,0:T(8,128)(2,1)S(1)} %slice.19), channel_id=1, source_target_pairs={{98,2},{27,3},{100,4},{29,5},{102,6},{31,7},{106,10},{3,11},{108,1... | collective-permute-start | bytes 1572872 | tf_op jit(solution)/shard_map/ppermute | solution.py:241
  93.9 1.3 collective-permute-start.7
  95.2 8.0 %collective-permute-done.12.refs_4_ = bf16[2,4,32,1024]{3,2,1,0:T(8,128)(2,1)S(1)} collective-permute-done((bf16[2,4,32,1024]{3,2,1,0:T(8,128)(2,1)S(1)}, bf16[2,4,32,1024]{3,2,1,0:T(8,128)(2,1)S(1)}, u32[]{:S(2)}, u32[]{:S(2)}) %collective-permute-start.12) | collective-permute-done | bytes 524320 | tf_op jit(solution)/shard_map/ppermute | solution.py:241
  103.2 1.2 collective-permute-start.16
  104.4 0.1 collective-permute-start.17
  104.5 1.5 collective-permute-start.9
  106.0 1.3 collective-permute-start.21
  107.3 22.3 %all-gather.5.cloned.1.call-done = bf16[128,32,1024]{2,1,0:T(8,128)(2,1)} async-done(((bf16[4,32,1024]{2,1,0:T(8,128)(2,1)}), bf16[128,32,1024]{2,1,0:T(8,128)(2,1)}) %all-gather.5.cloned.1.call-update) | async-done | bytes 8388624 | tf_op jit(solution)/shard_map/all_gather | solution.py:255
  129.6 3.3 %collective-permute-start.8 = (bf16[2,192,1024]{2,1,0:T(8,128)(2,1)}, bf16[2,192,1024]{2,1,0:T(8,128)(2,1)}, u32[]{:S(2)}, u32[]{:S(2)}) collective-permute-start(bf16[2,192,1024]{2,1,0:T(8,128)(2,1)} %collective-permute-done.7.to_3), channel_id=1, source_target_pairs={{6,4},{7,5},{14,12},{15,13},{22,20},{23,21},{30,28},{31,29},{38,36... | collective-permute-start | bytes 2359304 | tf_op jit(solution)/shard_map/ppermute | solution.py:228
  132.9 0.8 copy-done.5
  133.7 1.6 finish1.2.refs_0_.refs_12_
  135.3 1.6 collective-permute-start.18
  136.9 2.2 collective-permute-start.22
  139.1 1.8 finish1.3.refs_1_.refs_12_
  141.0 2.0 partial.1
  143.0 1.3 collective-permute-start.20
  144.3 1.5 collective-permute-start.23
  145.9 3.1 %collective-permute-done.8.to_2 = bf16[2,192,1024]{2,1,0:T(8,128)(2,1)} collective-permute-done((bf16[2,192,1024]{2,1,0:T(8,128)(2,1)}, bf16[2,192,1024]{2,1,0:T(8,128)(2,1)}, u32[]{:S(2)}, u32[]{:S(2)}) %collective-permute-start.8) | collective-permute-done | bytes 786464 | tf_op jit(solution)/shard_map/ppermute | solution.py:228
  149.0 8.0 %update.2.r = f32[2,192,1024]{2,1,0:T(8,128)} custom-call(s32[4]{0:T(128)} %pad_add_fusion.info, bf16[2,16,4,32,1024]{4,3,2,1,0:T(8,128)(2,1)} %bitcast.28, f32[2,192,1024]{2,1,0:T(8,128)} %get-tuple-element.24.r, bf16[2,192,1024]{2,1,0:T(8,128)(2,1)} %collective-permute-done.7.to_3, bf16[2,192,1024]{2,1,0:T(8,128)(2,1)} %collective-permute-done.8.to_2), custom_call_target="tpu_custom_call" | custom-call | bytes 1024 | tf_op jit(solution)/shard_map/update/pallas_call | solution.py:339
  157.0 1.7 finish2.2.refs_13_
  158.7 1.3 collective-permute-start.19
  160.0 5.9 %collective-permute-done.22.to_2 = bf16[2,192,1024]{2,1,0:T(8,128)(2,1)} collective-permute-done((bf16[2,192,1024]{2,1,0:T(8,128)(2,1)}, bf16[2,192,1024]{2,1,0:T(8,128)(2,1)}, u32[]{:S(2)}, u32[]{:S(2)}) %collective-permute-start.22) | collective-permute-done | bytes 786464 | tf_op jit(solution)/shard_map/ppermute | solution.py:228
  165.8 8.1 %update.3.r = f32[2,192,1024]{2,1,0:T(8,128)} custom-call(s32[4]{0:T(128)} %pad_add_fusion.info, bf16[2,16,4,32,1024]{4,3,2,1,0:T(8,128)(2,1)} %bitcast.29, f32[2,192,1024]{2,1,0:T(8,128)} %get-tuple-element.26.r, bf16[2,192,1024]{2,1,0:T(8,128)(2,1)} %collective-permute-done.21.to_3, bf16[2,192,1024]{2,1,0:T(8,128)(2,1)} %collective-permute-done.22.to_2), custom_call_target="tpu_custom_call" | custom-call | bytes 1024 | tf_op jit(solution)/shard_map/update/pallas_call | solution.py:339
  174.0 1.7 finish2.3.refs_13_
  175.7 1.3 collective-permute-start.24
  177.0 16.2 %collective-permute-done.19.a = bf16[2,192,1024]{2,1,0:T(8,128)(2,1)} collective-permute-done((bf16[2,192,1024]{2,1,0:T(8,128)(2,1)}, bf16[2,192,1024]{2,1,0:T(8,128)(2,1)}, u32[]{:S(2)}, u32[]{:S(2)}) %collective-permute-start.19) | collective-permute-done | bytes 786464 | tf_op jit(solution)/shard_map/ppermute | solution.py:228
  193.2 9.5 %collective-permute-done.20.refs_10_ = bf16[2,384,1024]{2,1,0:T(8,128)(2,1)S(1)} collective-permute-done((bf16[2,384,1024]{2,1,0:T(8,128)(2,1)}, bf16[2,384,1024]{2,1,0:T(8,128)(2,1)S(1)}, u32[]{:S(2)}, u32[]{:S(2)}) %collective-permute-start.20) | collective-permute-done | bytes 1572896 | tf_op jit(solution)/shard_map/ppermute | solution.py:228
  202.7 1.2 copy-done.7
  203.9 12.1 %finish3.2 = (bf16[192,1024]{1,0:T(8,128)(2,1)}, bf16[192,1024]{1,0:T(8,128)(2,1)}) custom-call(s32[4]{0:T(128)} %pad_add_fusion.info, f32[2,192,1024]{2,1,0:T(8,128)} %update.2.r, bf16[2,192,1024]{2,1,0:T(8,128)(2,1)} %collective-permute-done.19.a, bf16[2,16,160,1024]{3,2,1,0:T(8,128)(2,1)} %bitcast.25, bf16[2,512,512]{2,1,0:T(8,128)(2,1)} %bitcast.36, ...), custom_call_target="tpu_custom_call" | custom-call | flops 3000000000 | bytes 1024 | tf_op jit(solution)/shard_map/finish3/pallas_call | solution.py:312
  216.0 0.9 copy-done.9
  216.9 11.7 %finish3.3 = (bf16[192,1024]{1,0:T(8,128)(2,1)}, bf16[192,1024]{1,0:T(8,128)(2,1)}) custom-call(s32[4]{0:T(128)} %pad_add_fusion.info, f32[2,192,1024]{2,1,0:T(8,128)} %update.3.r, bf16[2,192,1024]{2,1,0:T(8,128)(2,1)} %copy-done.9, bf16[2,16,160,1024]{3,2,1,0:T(8,128)(2,1)} %bitcast.26, bf16[2,512,512]{2,1,0:T(8,128)(2,1)} %bitcast.37, ...), custom_call_target="tpu_custom_call" | custom-call | flops 3000000000 | bytes 1024 | tf_op jit(solution)/shard_map/finish3/pallas_call | solution.py:312
  228.7 0.5 collective-permute-start.25
  229.2 1.4 collective-permute-done.26
  230.6 0.6 collective-permute-done.25
  231.2 2.6 %maximum_select_fusion = bf16[768,1024]{1,0:T(8,128)(2,1)} fusion(bf16[192,1024]{1,0:T(8,128)(2,1)S(1)} %collective-permute-done.26, bf16[192,1024]{1,0:T(8,128)(2,1)S(1)} %collective-permute-done.25, bf16[192,1024]{1,0:T(8,128)(2,1)} %get-tuple-element.32, bf16[192,1024]{1,0:T(8,128)(2,1)S(1)} %copy-done.10, pred[]{:T(512)S(6)} %eq.6), kind=kLoop, calls=%fused_computation | loop fusion | flops 13369344 | bytes 3145729 | tf_op jit(solution)/shard_map/jit(_where)/select_n | solution.py:370
  (42 shorter events, 0.3 us)
Async XLA Ops:
  6.5 68.9 %copy-start = (bf16[768,1024]{1,0:T(8,128)(2,1)S(1)}, bf16[768,1024]{1,0:T(8,128)(2,1)}, u32[]{:S(2)}) copy-start(bf16[768,1024]{1,0:T(8,128)(2,1)} %param.4) | copy-start | bytes 4718596
  6.5 2.8 %copy-start.8 = (bf16[1024,16,32]{0,2,1:T(8,128)(2,1)S(1)}, bf16[1024,16,32]{0,2,1:T(8,128)(2,1)}, u32[]{:S(2)}) copy-start(bf16[1024,16,32]{0,2,1:T(8,128)(2,1)} %param.6) | copy-start | bytes 3145732
  6.5 74.2 %all-gather.7.cloned.1.call-start = ((), (), s32[]{:S(2)}) async-start(), calls=%async_computation.1 | async-start | bytes 10813440 | tf_op jit(solution)/shard_map/all_gather | solution.py:255
  9.3 120.3 %all-gather.5.cloned.1.call-start = ((), (), s32[]{:S(2)}) async-start(), calls=%async_computation | async-start | bytes 8650752 | tf_op jit(solution)/shard_map/all_gather | solution.py:255
  9.4 9.5 %collective-permute-start = (bf16[4,32,1024]{2,1,0:T(8,128)(2,1)S(1)}, bf16[4,32,1024]{2,1,0:T(8,128)(2,1)S(1)}, u32[]{:S(2)}, u32[]{:S(2)}) collective-permute-start(bf16[4,32,1024]{2,1,0:T(8,128)(2,1)S(1)} %get-tuple-element.38), channel_id=1, source_target_pairs={{10,2},{35,3},{12,4},{37,5},{14,6},{39,7},{18,10},{43,11},{20,12},... | collective-permute-start | bytes 786440 | tf_op jit(solution)/shard_map/ppermute | solution.py:241
  14.1 8.9 %collective-permute-start.1 = (bf16[4,32,1024]{2,1,0:T(8,128)(2,1)S(1)}, bf16[4,32,1024]{2,1,0:T(8,128)(2,1)S(1)}, u32[]{:S(2)}, u32[]{:S(2)}) collective-permute-start(bf16[4,32,1024]{2,1,0:T(8,128)(2,1)S(1)} %get-tuple-element.38), channel_id=1, source_target_pairs={{18,2},{67,3},{20,4},{69,5},{22,6},{71,7},{26,10},{75,11},{28,12},... | collective-permute-start | bytes 786440 | tf_op jit(solution)/shard_map/ppermute | solution.py:241
  16.3 10.5 %collective-permute-start.2 = (bf16[4,32,1024]{2,1,0:T(8,128)(2,1)S(1)}, bf16[4,32,1024]{2,1,0:T(8,128)(2,1)S(1)}, u32[]{:S(2)}, u32[]{:S(2)}) collective-permute-start(bf16[4,32,1024]{2,1,0:T(8,128)(2,1)S(1)} %get-tuple-element.38), channel_id=1, source_target_pairs={{26,2},{99,3},{28,4},{101,5},{30,6},{103,7},{2,10},{107,11},{4,12}... | collective-permute-start | bytes 786440 | tf_op jit(solution)/shard_map/ppermute | solution.py:241
  26.9 4.5 %copy-start.2 = (bf16[4,4,32,1024]{3,2,1,0:T(8,128)(2,1)}, bf16[4,4,32,1024]{3,2,1,0:T(8,128)(2,1)S(1)}, u32[]{:S(2)}) copy-start(bf16[4,4,32,1024]{3,2,1,0:T(8,128)(2,1)S(1)} %pad_maximum_fusion.refs_0_) | copy-start | bytes 3145732
  26.9 18.0 %collective-permute-start.3 = (bf16[4,4,32,1024]{3,2,1,0:T(8,128)(2,1)S(1)}, bf16[4,4,32,1024]{3,2,1,0:T(8,128)(2,1)}, u32[]{:S(2)}, u32[]{:S(2)}) collective-permute-start(bf16[4,4,32,1024]{3,2,1,0:T(8,128)(2,1)S(1)} %pad_maximum_fusion.refs_0_), channel_id=1, source_target_pairs={{34,2},{11,3},{36,4},{13,5},{38,6},{15,7},{42,10},{19,11},{44,12},... | collective-permute-start | bytes 3145736 | tf_op jit(solution)/shard_map/ppermute | solution.py:241
  31.5 20.0 %collective-permute-start.4 = (bf16[4,4,32,1024]{3,2,1,0:T(8,128)(2,1)S(1)}, bf16[4,4,32,1024]{3,2,1,0:T(8,128)(2,1)}, u32[]{:S(2)}, u32[]{:S(2)}) collective-permute-start(bf16[4,4,32,1024]{3,2,1,0:T(8,128)(2,1)S(1)} %pad_maximum_fusion.refs_0_), channel_id=1, source_target_pairs={{98,2},{27,3},{100,4},{29,5},{102,6},{31,7},{106,10},{3,11},{108,1... | collective-permute-start | bytes 3145736 | tf_op jit(solution)/shard_map/ppermute | solution.py:241
  51.5 4.6 %collective-permute-start.5 = (bf16[4,32,1024]{2,1,0:T(8,128)(2,1)S(1)}, bf16[4,32,1024]{2,1,0:T(8,128)(2,1)S(1)}, u32[]{:S(2)}, u32[]{:S(2)}) collective-permute-start(bf16[4,32,1024]{2,1,0:T(8,128)(2,1)S(1)} %get-tuple-element.20), channel_id=1, source_target_pairs={{6,2},{7,3},{14,10},{15,11},{22,18},{23,19},{30,26},{31,27},{38,34... | collective-permute-start | bytes 786440 | tf_op jit(solution)/shard_map/ppermute | solution.py:228
  56.1 0.7 copy-start.11
  60.1 20.6 %copy-start.1 = (bf16[2,512,512]{1,2,0:T(8,128)(2,1)}, bf16[2,512,512]{1,2,0:T(8,128)(2,1)S(1)}, u32[]{:S(2)}) copy-start(bf16[2,512,512]{1,2,0:T(8,128)(2,1)S(1)} %copy.6) | copy-start | bytes 3145732
  60.1 20.6 %collective-permute-start.6 = (bf16[2,512,512]{2,1,0:T(8,128)(2,1)S(1)}, bf16[2,512,512]{2,1,0:T(8,128)(2,1)}, u32[]{:S(2)}, u32[]{:S(2)}) collective-permute-start(bf16[2,512,512]{2,1,0:T(8,128)(2,1)S(1)} %bitcast.30), channel_id=1, source_target_pairs={{0,1},{1,0},{2,3},{3,2},{4,5},{5,4},{6,7},{7,6},{8,9},{9,8},{10,11... | collective-permute-start | bytes 3145736 | tf_op jit(solution)/shard_map/ppermute | solution.py:231
  75.3 15.1 %collective-permute-start.13 = (bf16[4,4,32,1024]{3,2,1,0:T(8,128)(2,1)}, bf16[4,4,32,1024]{3,2,1,0:T(8,128)(2,1)}, u32[]{:S(2)}, u32[]{:S(2)}) collective-permute-start(bf16[4,4,32,1024]{3,2,1,0:T(8,128)(2,1)} %copy-done.2), channel_id=1, source_target_pairs={{0,1},{1,0},{2,3},{3,2},{4,5},{5,4},{6,7},{7,6},{8,9},{9,8},{10,11... | collective-permute-start | bytes 3145736 | tf_op jit(solution)/shard_map/ppermute | solution.py:231
  78.2 15.6 %collective-permute-start.11 = (bf16[2,4,32,1024]{3,2,1,0:T(8,128)(2,1)}, bf16[2,4,32,1024]{3,2,1,0:T(8,128)(2,1)S(1)}, u32[]{:S(2)}, u32[]{:S(2)}) collective-permute-start(bf16[2,4,32,1024]{3,2,1,0:T(8,128)(2,1)} %slice.18), channel_id=1, source_target_pairs={{34,2},{11,3},{36,4},{13,5},{38,6},{15,7},{42,10},{19,11},{44,12},... | collective-permute-start | bytes 1572872 | tf_op jit(solution)/shard_map/ppermute | solution.py:241
  80.2 24.2 %collective-permute-start.14 = (bf16[4,4,32,1024]{3,2,1,0:T(8,128)(2,1)}, bf16[4,4,32,1024]{3,2,1,0:T(8,128)(2,1)}, u32[]{:S(2)}, u32[]{:S(2)}) collective-permute-start(bf16[4,4,32,1024]{3,2,1,0:T(8,128)(2,1)} %collective-permute-done.3.refs_1_), channel_id=1, source_target_pairs={{0,1},{1,0},{2,3},{3,2},{4,5},{5,4},{6,7},{7,6},{8,9},{9,8},{10,11... | collective-permute-start | bytes 3145736 | tf_op jit(solution)/shard_map/ppermute | solution.py:231
  80.7 23.8 %collective-permute-start.15 = (bf16[4,4,32,1024]{3,2,1,0:T(8,128)(2,1)}, bf16[4,4,32,1024]{3,2,1,0:T(8,128)(2,1)}, u32[]{:S(2)}, u32[]{:S(2)}) collective-permute-start(bf16[4,4,32,1024]{3,2,1,0:T(8,128)(2,1)} %collective-permute-done.4.refs_2_), channel_id=1, source_target_pairs={{0,1},{1,0},{2,3},{3,2},{4,5},{5,4},{6,7},{7,6},{8,9},{9,8},{10,11... | collective-permute-start | bytes 3145736 | tf_op jit(solution)/shard_map/ppermute | solution.py:231
  87.8 18.2 %collective-permute-start.10 = (bf16[2,192,1024]{2,1,0:T(8,128)(2,1)}, bf16[2,192,1024]{2,1,0:T(8,128)(2,1)}, u32[]{:S(2)}, u32[]{:S(2)}) collective-permute-start(bf16[2,192,1024]{2,1,0:T(8,128)(2,1)} %get-tuple-element.25.refs_11_), channel_id=1, source_target_pairs={{0,2},{1,3},{8,10},{9,11},{16,18},{17,19},{24,26},{25,27},{32,34},... | collective-permute-start | bytes 2359304 | tf_op jit(solution)/shard_map/ppermute | solution.py:228
  90.5 12.7 %collective-permute-start.12 = (bf16[2,4,32,1024]{3,2,1,0:T(8,128)(2,1)S(1)}, bf16[2,4,32,1024]{3,2,1,0:T(8,128)(2,1)S(1)}, u32[]{:S(2)}, u32[]{:S(2)}) collective-permute-start(bf16[2,4,32,1024]{3,2,1,0:T(8,128)(2,1)S(1)} %slice.19), channel_id=1, source_target_pairs={{98,2},{27,3},{100,4},{29,5},{102,6},{31,7},{106,10},{3,11},{108,1... | collective-permute-start | bytes 1572872 | tf_op jit(solution)/shard_map/ppermute | solution.py:241
  93.8 39.1 %copy-start.3 = (bf16[2,4,32,1024]{3,2,1,0:T(8,128)(2,1)}, bf16[2,4,32,1024]{3,2,1,0:T(8,128)(2,1)S(1)}, u32[]{:S(2)}) copy-start(bf16[2,4,32,1024]{3,2,1,0:T(8,128)(2,1)S(1)} %collective-permute-done.11.refs_3_) | copy-start | bytes 1572868
  93.9 35.8 %collective-permute-start.7 = (bf16[2,192,1024]{2,1,0:T(8,128)(2,1)}, bf16[2,192,1024]{2,1,0:T(8,128)(2,1)}, u32[]{:S(2)}, u32[]{:S(2)}) collective-permute-start(bf16[2,192,1024]{2,1,0:T(8,128)(2,1)} %get-tuple-element.25.refs_11_), channel_id=1, source_target_pairs={{0,6},{1,7},{8,14},{9,15},{16,22},{17,23},{24,30},{25,31},{32,38},... | collective-permute-start | bytes 2359304 | tf_op jit(solution)/shard_map/ppermute | solution.py:228
  103.2 29.7 %copy-start.4 = (bf16[2,4,32,1024]{3,2,1,0:T(8,128)(2,1)}, bf16[2,4,32,1024]{3,2,1,0:T(8,128)(2,1)S(1)}, u32[]{:S(2)}) copy-start(bf16[2,4,32,1024]{3,2,1,0:T(8,128)(2,1)S(1)} %collective-permute-done.12.refs_4_) | copy-start | bytes 1572868
  103.2 29.7 %collective-permute-start.16 = (bf16[2,4,32,1024]{3,2,1,0:T(8,128)(2,1)S(1)}, bf16[2,4,32,1024]{3,2,1,0:T(8,128)(2,1)S(1)}, u32[]{:S(2)}, u32[]{:S(2)}) collective-permute-start(bf16[2,4,32,1024]{3,2,1,0:T(8,128)(2,1)S(1)} %collective-permute-done.11.refs_3_), channel_id=1, source_target_pairs={{0,1},{1,0},{2,3},{3,2},{4,5},{5,4},{6,7},{7,6},{8,9},{9,8},{10,11... | collective-permute-start | bytes 1572872 | tf_op jit(solution)/shard_map/ppermute | solution.py:231
  104.4 28.5 %collective-permute-start.17 = (bf16[2,4,32,1024]{3,2,1,0:T(8,128)(2,1)S(1)}, bf16[2,4,32,1024]{3,2,1,0:T(8,128)(2,1)}, u32[]{:S(2)}, u32[]{:S(2)}) collective-permute-start(bf16[2,4,32,1024]{3,2,1,0:T(8,128)(2,1)S(1)} %collective-permute-done.12.refs_4_), channel_id=1, source_target_pairs={{0,1},{1,0},{2,3},{3,2},{4,5},{5,4},{6,7},{7,6},{8,9},{9,8},{10,11... | collective-permute-start | bytes 1572872 | tf_op jit(solution)/shard_map/ppermute | solution.py:231
  104.5 32.5 %collective-permute-start.9 = (bf16[2,192,1024]{2,1,0:T(8,128)(2,1)}, bf16[2,192,1024]{2,1,0:T(8,128)(2,1)}, u32[]{:S(2)}, u32[]{:S(2)}) collective-permute-start(bf16[2,192,1024]{2,1,0:T(8,128)(2,1)} %get-tuple-element.22.refs_11_), channel_id=1, source_target_pairs={{0,2},{1,3},{8,10},{9,11},{16,18},{17,19},{24,26},{25,27},{32,34},... | collective-permute-start | bytes 2359304 | tf_op jit(solution)/shard_map/ppermute | solution.py:228
  106.0 30.9 %collective-permute-start.21 = (bf16[2,192,1024]{2,1,0:T(8,128)(2,1)}, bf16[2,192,1024]{2,1,0:T(8,128)(2,1)}, u32[]{:S(2)}, u32[]{:S(2)}) collective-permute-start(bf16[2,192,1024]{2,1,0:T(8,128)(2,1)} %get-tuple-element.22.refs_11_), channel_id=1, source_target_pairs={{0,6},{1,7},{8,14},{9,15},{16,22},{17,23},{24,30},{25,31},{32,38},... | collective-permute-start | bytes 2359304 | tf_op jit(solution)/shard_map/ppermute | solution.py:228
  129.6 19.4 %collective-permute-start.8 = (bf16[2,192,1024]{2,1,0:T(8,128)(2,1)}, bf16[2,192,1024]{2,1,0:T(8,128)(2,1)}, u32[]{:S(2)}, u32[]{:S(2)}) collective-permute-start(bf16[2,192,1024]{2,1,0:T(8,128)(2,1)} %collective-permute-done.7.to_3), channel_id=1, source_target_pairs={{6,4},{7,5},{14,12},{15,13},{22,20},{23,21},{30,28},{31,29},{38,36... | collective-permute-start | bytes 2359304 | tf_op jit(solution)/shard_map/ppermute | solution.py:228
  132.9 0.8 copy-start.5
  135.3 21.6 %collective-permute-start.18 = (bf16[2,192,1024]{2,1,0:T(8,128)(2,1)}, bf16[2,192,1024]{2,1,0:T(8,128)(2,1)}, u32[]{:S(2)}, u32[]{:S(2)}) collective-permute-start(bf16[2,192,1024]{2,1,0:T(8,128)(2,1)} %finish1.2.refs_0_.refs_12_), channel_id=1, source_target_pairs={{2,4},{3,5},{10,12},{11,13},{18,20},{19,21},{26,28},{27,29},{34,36... | collective-permute-start | bytes 2359304 | tf_op jit(solution)/shard_map/ppermute | solution.py:228
  136.9 28.9 %collective-permute-start.22 = (bf16[2,192,1024]{2,1,0:T(8,128)(2,1)}, bf16[2,192,1024]{2,1,0:T(8,128)(2,1)}, u32[]{:S(2)}, u32[]{:S(2)}) collective-permute-start(bf16[2,192,1024]{2,1,0:T(8,128)(2,1)} %collective-permute-done.21.to_3), channel_id=1, source_target_pairs={{6,4},{7,5},{14,12},{15,13},{22,20},{23,21},{30,28},{31,29},{38,36... | collective-permute-start | bytes 2359304 | tf_op jit(solution)/shard_map/ppermute | solution.py:228
  141.0 3.4 %copy-start.6 = (bf16[2,192,1024]{2,1,0:T(8,128)(2,1)S(1)}, bf16[2,192,1024]{2,1,0:T(8,128)(2,1)}, u32[]{:S(2)}) copy-start(bf16[2,192,1024]{2,1,0:T(8,128)(2,1)} %finish1.3.refs_1_.refs_12_) | copy-start | bytes 2359300
  143.0 59.6 %collective-permute-start.20 = (bf16[2,384,1024]{2,1,0:T(8,128)(2,1)}, bf16[2,384,1024]{2,1,0:T(8,128)(2,1)S(1)}, u32[]{:S(2)}, u32[]{:S(2)}) collective-permute-start(bf16[2,384,1024]{2,1,0:T(8,128)(2,1)} %partial.1), channel_id=1, source_target_pairs={{2,6},{3,7},{10,14},{11,15},{18,22},{19,23},{26,30},{27,31},{34,38... | collective-permute-start | bytes 4718600 | tf_op jit(solution)/shard_map/ppermute | solution.py:228
  144.3 29.6 %collective-permute-start.23 = (bf16[2,192,1024]{2,1,0:T(8,128)(2,1)S(1)}, bf16[2,192,1024]{2,1,0:T(8,128)(2,1)}, u32[]{:S(2)}, u32[]{:S(2)}) collective-permute-start(bf16[2,192,1024]{2,1,0:T(8,128)(2,1)S(1)} %copy-done.6), channel_id=1, source_target_pairs={{2,4},{3,5},{10,12},{11,13},{18,20},{19,21},{26,28},{27,29},{34,36... | collective-permute-start | bytes 2359304 | tf_op jit(solution)/shard_map/ppermute | solution.py:228
  158.7 34.5 %collective-permute-start.19 = (bf16[2,192,1024]{2,1,0:T(8,128)(2,1)}, bf16[2,192,1024]{2,1,0:T(8,128)(2,1)}, u32[]{:S(2)}, u32[]{:S(2)}) collective-permute-start(bf16[2,192,1024]{2,1,0:T(8,128)(2,1)} %finish2.2.refs_13_), channel_id=1, source_target_pairs={{4,6},{5,7},{12,14},{13,15},{20,22},{21,23},{28,30},{29,31},{36,38... | collective-permute-start | bytes 2359304 | tf_op jit(solution)/shard_map/ppermute | solution.py:228
  175.7 40.3 %collective-permute-start.24 = (bf16[2,192,1024]{2,1,0:T(8,128)(2,1)}, bf16[2,192,1024]{2,1,0:T(8,128)(2,1)S(1)}, u32[]{:S(2)}, u32[]{:S(2)}) collective-permute-start(bf16[2,192,1024]{2,1,0:T(8,128)(2,1)} %finish2.3.refs_13_), channel_id=1, source_target_pairs={{4,6},{5,7},{12,14},{13,15},{20,22},{21,23},{28,30},{29,31},{36,38... | collective-permute-start | bytes 2359304 | tf_op jit(solution)/shard_map/ppermute | solution.py:228
  202.7 1.2 copy-start.7
  216.0 0.9 copy-start.9
  216.9 14.3 %copy-start.10 = (bf16[192,1024]{1,0:T(8,128)(2,1)S(1)}, bf16[192,1024]{1,0:T(8,128)(2,1)}, u32[]{:S(2)}) copy-start(bf16[192,1024]{1,0:T(8,128)(2,1)} %get-tuple-element.29) | copy-start | bytes 1179652
  228.6 2.0 collective-permute-start.26
  228.7 2.5 %collective-permute-start.25 = (bf16[192,1024]{1,0:T(8,128)(2,1)}, bf16[192,1024]{1,0:T(8,128)(2,1)S(1)}, u32[]{:S(2)}, u32[]{:S(2)}) collective-permute-start(bf16[192,1024]{1,0:T(8,128)(2,1)} %get-tuple-element.33), channel_id=1, source_target_pairs={{0,1},{1,0},{2,3},{3,2},{4,5},{5,4},{6,7},{7,6},{8,9},{9,8},{10,11... | collective-permute-start | bytes 1179656 | tf_op jit(solution)/shard_map/ppermute | solution.py:231
Sparse Core Ops, SparseCore 0:
  9.6 67.1 all-gather.6
  79.1 50.4 all-gather.4

commit v3 on v2

v3 whole, which is shorter than its diff:
```python
import functools
import math

import jax
import jax.numpy as jnp
from jax import lax
from jax.experimental import pallas as pl
from jax.experimental.pallas import tpu as pltpu
from jax.sharding import PartitionSpec as P

CHUNKS = 2
SIDE = 4
LEAD = 64
SLAB = 32
BF = jnp.bfloat16
F32 = jnp.float32
ANY = pl.BlockSpec(memory_space=pl.ANY)
SMEM = pl.BlockSpec(memory_space=pltpu.SMEM)
VMEM = pl.BlockSpec(memory_space=pltpu.VMEM)


def mm(a, b):
    return jnp.dot(a, b, preferred_element_type=F32)


def after(x, *deps):
    return lax.optimization_barrier((x, *deps))[0]


def start_diag(info, head, dt_own, dt_oth, gv, dv, sem):
    core = info[1]
    depth = gv.shape[2]
    pltpu.make_async_copy(head.at[:, :, pl.ds(LEAD, depth)], gv, sem.at[0]).start()
    pltpu.make_async_copy(dt_own, dv.at[core], sem.at[1]).start()
    pltpu.make_async_copy(dt_oth, dv.at[1 - core], sem.at[1]).start()


def wait_diag(gv, dv, sem):
    pltpu.make_async_copy(gv, gv, sem.at[0]).wait()
    pltpu.make_async_copy(dv, dv, sem.at[1]).wait()


def solve(running, diag, dt, f):
    size = dt.shape[-1]

    def column(i):
        return running[i // 2, :, (i % 2) * size:(i % 2 + 1) * size]

    def store(i, value):
        f[i // 2, :, (i % 2) * size:(i % 2 + 1) * size] = value

    def left(i, k):
        block = diag[i // 2, :, k * SLAB:(k + 1) * SLAB, (i % 2) * size:(i % 2 + 1) * size]
        return block.reshape(size, size)

    f0 = mm(column(0).astype(BF), dt[0, 0]).astype(BF)
    store(0, f0)
    f1 = mm((column(1) - mm(f0, left(1, 0))).astype(BF), dt[0, 1]).astype(BF)
    store(1, f1)
    f2 = mm((column(2) - mm(f0, left(2, 0)) - mm(f1, left(2, 1))).astype(BF), dt[1, 0]).astype(BF)
    store(2, f2)
    f3 = column(3) - mm(f0, left(3, 0)) - mm(f1, left(3, 1)) - mm(f2, left(3, 2))
    store(3, mm(f3.astype(BF), dt[1, 1]).astype(BF))


def hold_kernel(x, token, out):
    pass


def pick_kernel(info, first, other, out):
    out[...] = jnp.where(info[0] == 1, first[...], other[...])


def scores_kernel(scale, info, emb, dt_own, dt_oth, head, out, f, lm, gv, dv, sem):
    plane = info[0]
    lead = lm.shape[2]
    copies = [pltpu.make_async_copy(head.at[i, :, pl.ds(0, lead)], lm.at[i], sem.at[2 + i]) for i in range(2)]
    for copy in copies:
        copy.start()
    pl.when(plane == 0)(lambda: start_diag(info, head, dt_own, dt_oth, gv, dv, sem))
    for half in range(2):
        copies[half].wait()
        points = lm[half].reshape(emb.shape[1], lm.shape[3])
        out[half] = jnp.exp(mm(emb[...], points) * scale)

    @pl.when(plane == 0)
    def _():
        wait_diag(gv, dv, sem)
        solve(out, gv, dv, f)


def start_factor(factor, lv, sems):
    depth = lv.shape[2]
    copies = []
    for half in range(2):
        part = factor.at[half, :, pl.ds(factor.shape[2] - depth, depth)]
        copies.append(pltpu.make_async_copy(part, lv.at[half], sems.at[half]))
        copies[-1].start()
    return copies


def subtract(acc, av, lv, copies):
    size = lv.shape[1] * SLAB
    for half in range(2):
        copies[half].wait()
        for k in range(lv.shape[2] // SLAB):
            left = av[k // 2, :, (k % 2) * size:(k % 2 + 1) * size]
            acc[half] -= mm(left, lv[half, :, k * SLAB:(k + 1) * SLAB].reshape(size, -1))


def finish_kernel(role, info, r, a, head, dt_own, dt_oth, factor, *refs):
    last = role == SIDE - 1
    if last:
        part, earlier, refs = refs[0], refs[1:SIDE], refs[SIDE:]
        keep, give, f, pv, acc, av, lv, gv, dv, sems, sem = refs
    else:
        f, acc, av, lv, gv, dv, sems, sem = refs
    plane, core = info[0], info[1]

    @pl.when(plane == role)
    def _():
        ca = pltpu.make_async_copy(a, av, sems.at[2])
        cr = pltpu.make_async_copy(r, acc, sems.at[3])
        ca.start()
        cr.start()
        copies = start_factor(factor, lv, sems)
        start_diag(info, head, dt_own, dt_oth, gv, dv, sem)
        if last:
            cp = pltpu.make_async_copy(part, pv, sems.at[6])
            cp.start()
        ca.wait()
        cr.wait()
        if last:
            cp.wait()
            acc[...] += pv[...].astype(F32)
        subtract(acc, av, lv, copies)
        wait_diag(gv, dv, sem)
        solve(acc, gv, dv, f)
        if last:
            keep[...] = f[pl.ds(core, 1)][0]
            give[...] = f[pl.ds(1 - core, 1)][0]

    if last:
        for z, done in enumerate(earlier):

            @pl.when(plane == z)
            def _():
                c0 = pltpu.make_async_copy(done.at[core], keep, sems.at[0])
                c1 = pltpu.make_async_copy(done.at[1 - core], give, sems.at[1])
                c0.start()
                c1.start()
                c0.wait()
                c1.wait()


def partial_kernel(info, factor, own, p, acc, av, lv, sems):
    @pl.when(info[0] == 1)
    def _():
        ca = pltpu.make_async_copy(own, av, sems.at[2])
        ca.start()
        copies = start_factor(factor, lv, sems)
        acc[...] = jnp.zeros_like(acc)
        ca.wait()
        subtract(acc, av, lv, copies)
        p[...] = acc[...].astype(BF)


def update_kernel(info, head, r, to_3, to_2, r_out, acc, av, lv, sems):
    @pl.when(info[0] >= 2)
    def _():
        copies = start_factor(head, lv, sems)
        cr = pltpu.make_async_copy(r, acc, sems.at[2])
        cr.start()
        for plane, a in ((2, to_2), (3, to_3)):
            pl.when(info[0] == plane)(lambda a=a: pltpu.make_async_copy(a, av, sems.at[3]).start())
        cr.wait()
        pltpu.make_async_copy(to_2, av, sems.at[3]).wait()
        subtract(acc, av, lv, copies)
        out = pltpu.make_async_copy(acc, r_out, sems.at[2])
        out.start()
        out.wait()


def params(mib=60):
    return pltpu.CompilerParams(vmem_limit_bytes=mib << 20)


def cost(us):
    return pl.CostEstimate(flops=int(us * 1e9), bytes_accessed=1 << 10, transcendentals=0)


def per_device(embeddings, landmarks, factor_rows, diag_inverse):
    tokens, depth = embeddings.shape
    rows = lax.axis_size("rows")
    planes = lax.axis_size("cols") // 2
    here = lax.axis_index("cols")
    plane, core = here // 2, here % 2
    row = lax.axis_index("rows")
    own_rows, blocks, slab = factor_rows.shape
    size = diag_inverse.shape[1]
    lead = landmarks.shape[1]
    n = CHUNKS
    half = tokens // 2
    t = half // n
    scale = 0.5 / math.sqrt(depth)
    per_plane = blocks // planes
    info = jnp.stack([plane, core, row // SIDE, row % SIDE]).astype(jnp.int32)

    def send(x, source, target):
        return lax.ppermute(x, "cols", [(2 * source + k, 2 * target + k) for k in range(2)])

    def swap(x):
        return lax.ppermute(x, "cols", [(c, c ^ 1) for c in range(2 * planes)])

    ft = factor_rows.transpose(1, 2, 0)
    groups = [[r * 2 * planes + 2 * z + k for k in range(2) for r in range(rows)] for z in range(planes)]

    def gather(x):
        everyone = lax.all_gather(x, ("rows", "cols"), axis=0, axis_index_groups=groups)
        return everyone.reshape(2, rows, *x.shape)

    diag = lax.dynamic_slice_in_dim(ft, per_plane * plane, per_plane - 1, 0)
    head = gather(
        jnp.concatenate([landmarks.T, diag.reshape(-1, own_rows), ft[:per_plane].reshape(-1, own_rows)], axis=0)
    )
    dt_own = diag_inverse.transpose(0, 2, 1)
    dt_oth = swap(dt_own)

    first = send(ft[per_plane:2 * per_plane], 3, 1)
    other = lax.dynamic_slice_in_dim(ft, per_plane * jnp.maximum(plane - 1, 0), per_plane, 0)
    factor = gather(
        pl.pallas_call(
            pick_kernel,
            in_specs=[SMEM, VMEM, VMEM],
            out_specs=VMEM,
            out_shape=jax.ShapeDtypeStruct((per_plane * slab, own_rows), BF),
            cost_estimate=cost(0),
            name="pick",
        )(info, first.reshape(-1, own_rows), other.reshape(-1, own_rows))
    )

    emb = lax.dynamic_slice_in_dim(embeddings, core * half, half, 0)
    chunk_f32 = jax.ShapeDtypeStruct((2, t, own_rows), F32)
    chunk_bf = jax.ShapeDtypeStruct((2, t, own_rows), BF)
    whole_bf = jax.ShapeDtypeStruct((2, half, own_rows), BF)
    diag_scratch = [
        pltpu.VMEM((2, rows, (per_plane - 1) * slab, own_rows), BF),
        pltpu.VMEM((2, 2, size, size), BF),
    ]
    factor_scratch = [
        pltpu.VMEM(chunk_f32.shape, F32),
        pltpu.VMEM(chunk_bf.shape, BF),
        pltpu.VMEM((2, rows, per_plane * slab, own_rows), BF),
        pltpu.SemaphoreType.DMA((7,)),
    ]
    r, f0 = [], []
    for q in range(n):
        x = emb[q * t:(q + 1) * t]
        out = pl.pallas_call(
            functools.partial(scores_kernel, scale),
            in_specs=[SMEM, VMEM] + [ANY] * 3,
            out_specs=[VMEM] * 2,
            out_shape=[chunk_f32, chunk_bf],
            scratch_shapes=[pltpu.VMEM((2, rows, lead, own_rows), BF)]
            + diag_scratch
            + [pltpu.SemaphoreType.DMA((4,))],
            compiler_params=params(),
            cost_estimate=cost(100),
            name="scores",
        )(info, after(x, f0[-1]) if q else x, dt_own, dt_oth, head)
        r.append(out[0])
        f0.append(out[1])
    f0_to_1 = [send(x, 0, 1) for x in f0]
    f0_to_3 = [send(x, 0, 3) for x in f0]
    f0_to_2 = [send(x, 3, 2) for x in f0_to_3]
    r[0] = pl.pallas_call(
        hold_kernel,
        in_specs=[ANY, ANY],
        out_specs=ANY,
        out_shape=chunk_f32,
        input_output_aliases={0: 0},
        cost_estimate=cost(100),
        name="hold",
    )(r[0], f0[-1])

    def finish(role, r, a, more=()):
        last = role == planes - 1
        one = jax.ShapeDtypeStruct((t, own_rows), BF)
        return pl.pallas_call(
            functools.partial(finish_kernel, role),
            in_specs=[SMEM] + [ANY] * (6 + len(more)),
            out_specs=[VMEM] * 2 if last else VMEM,
            out_shape=[one, one] if last else chunk_bf,
            scratch_shapes=([pltpu.VMEM(chunk_bf.shape, BF)] * 2 if last else [])
            + factor_scratch[:3]
            + diag_scratch
            + [factor_scratch[3], pltpu.SemaphoreType.DMA((2,))],
            compiler_params=params(),
            cost_estimate=cost(0.8),
            name=f"finish{role}",
        )(info, r, a, head, dt_own, dt_oth, head if role == 1 else factor, *more)

    def partial(own):
        return pl.pallas_call(
            partial_kernel,
            in_specs=[SMEM] + [ANY] * 2,
            out_specs=VMEM,
            out_shape=chunk_bf,
            scratch_shapes=factor_scratch,
            compiler_params=params(),
            cost_estimate=cost(0),
            name="partial",
        )(info, factor, own)

    def update(r, to_3, to_2):
        return pl.pallas_call(
            update_kernel,
            in_specs=[SMEM] + [ANY] * 4,
            out_specs=ANY,
            out_shape=chunk_f32,
            scratch_shapes=factor_scratch,
            compiler_params=params(),
            cost_estimate=cost(0),
            name="update",
        )(info, head, r, to_3, to_2)

    f1, parts = [], []
    for q in range(n):
        f1.append(finish(1, r[q], after(f0_to_1[q], *f1)))
    f1_to_2 = [send(x, 1, 2) for x in f1]
    r2, f2 = [], []
    for q in range(n):
        r2.append(update(r[q], f0_to_3[q], after(f0_to_2[q], f1[-1], *f2)))
        if q == 0:
            for i in range(n):
                parts.append(partial(after(f1[i], r2[0], *parts)))
        f2.append(finish(2, r2[q], f1_to_2[q]))
    parts = [send(x, 1, 3) for x in parts]
    f2_to_3 = [send(x, 2, 3) for x in f2]
    done = []
    for q in range(n):
        a = after(f2_to_3[q], *[x[0] for x in done])
        done.append(finish(3, r2[q], a, (parts[q], f0[q], f1[q], f2[q])))
    keep = [x for x, _ in done]
    got = [swap(x) for _, x in done]
    return jnp.where(core == 0, jnp.concatenate(keep + got, axis=0), jnp.concatenate(got + keep, axis=0))


def solution(mesh):
    in_specs = (P("rows", None), P("cols", "rows"), P("cols", None, "rows"), P("cols", None, None))
    out_specs = P("rows", "cols")
    return jax.shard_map(
        per_device, mesh=mesh, in_specs=in_specs, out_specs=out_specs, check_vma=False
    )
```

time: 241 us -> 227 us (0.942)
  starting transfers between devices: 58.5 us -> 20.4 us
  waiting for transfers between devices: 94.8 us -> 112 us
  Pallas kernels: 57.6 us -> 61.4 us
  local copies, waits for them, and re-layouts: 10.9 us -> 14.2 us
    all_gather x2, waiting for transfers between devices: 22.3 us -> 67.4 us  [gather(): lax.all_gather(x, ('rows', 'cols'), axis=0, axis_index_groups=groups)]
    ppermute x7 -> x0, waiting for transfers between devices: 33.2 us -> none  [fetch(): return lax.ppermute(x, ('rows', 'cols'), pairs)]
    ppermute x7 -> x0, starting transfers between devices: 21.2 us -> none  [fetch(): return lax.ppermute(x, ('rows', 'cols'), pairs)]
    ppermute x8 -> x3, starting transfers between devices: 17.7 us -> 3.23 us  [swap(): return lax.ppermute(x, 'cols', [(c, c ^ 1) for c in range(2 * planes)])]
    ppermute x12 -> x13, waiting for transfers between devices: 37.3 us -> 43.2 us  [send(): lax.ppermute(x, 'cols', [(2 * source + k, 2 * target + k) for k in range(...]
    pallas_call x1 -> x2, Pallas kernels: 7.03 us -> 10.7 us  [per_device(): pl.pallas_call(functools.partial(scores_kernel, scale), in_specs=[SMEM, V...]
    unnamed x25 -> x33, local copies, waits for them, and re-layouts: 5.12 us -> 8.38 us
    ppermute x12 -> x13, starting transfers between devices: 19.5 us -> 17.1 us  [send(): lax.ppermute(x, 'cols', [(2 * source + k, 2 * target + k) for k in range(...]
  transfers between devices with their start and end apart: 29 -> 18, of which waited for: 13 -> 8; matrix products, arithmetic and copies ran while one was open for 3% -> 2% of each run, Pallas kernels for 19% -> 22%
where the time goes in v3:
time: 227 us; the launch traced here: 226 us
  waiting for transfers between devices  112 us (49%)
  Pallas kernels  61.4 us (27%)
  starting transfers between devices  20.4 us (9%)
  local copies, waits for them, and re-layouts  14.2 us (6%)
  between operations  13.8 us (6%)
  other arithmetic  4.1 us (2%)
    all_gather x2, waiting for transfers between devices, gather(): lax.all_gather(x, ('rows', 'cols'), axis=0, axis_index_groups=groups)  67.4 us
    ppermute x13, waiting for transfers between devices, send(): lax.ppermute(x, 'cols', [(2 * source + k, 2 * target + k) for k in range(...  43.2 us
    pallas_call x6, Pallas kernels, finish(): pl.pallas_call(functools.partial(finish_kernel, role), in_specs=[SMEM] +...  29.5 us
    ppermute x13, starting transfers between devices, send(): lax.ppermute(x, 'cols', [(2 * source + k, 2 * target + k) for k in range(...  17.1 us
    pallas_call x2, Pallas kernels, update(): pl.pallas_call(update_kernel, in_specs=[SMEM] + [ANY] * 4, out_specs=ANY,...  16 us
    pallas_call x2, Pallas kernels, per_device(): pl.pallas_call(functools.partial(scores_kernel, scale), in_specs=[SMEM, V...  10.7 us
    unnamed x33, local copies, waits for them, and re-layouts  8.38 us
  transfers between devices with their start and end apart: 18, of which 8 were waited for; matrix products, arithmetic and copies ran while one was open for 2% of the time, Pallas kernels for 22%

profile of v3, /device:TPU:97, one launch (start us, length us, event | category | flops | bytes accessed | tf_op | source)
XLA Modules:
  0.0 226.3 jit_solution(3628362160306732867)
XLA Ops:
  6.5 1.0 constant_dynamic-slice_fusion.3
  7.6 1.1 fusion
  8.7 0.9 pad_maximum_fusion
  9.5 0.0 all-gather.5.cloned.1.call-update
  9.5 0.0 all-gather.7.cloned.1.call-start
  9.6 0.5 copy.6
  10.2 0.8 collective-permute-start
  10.9 2.2 collective-permute-start.6
  13.1 0.6 pad_add_fusion.info
  13.7 1.7 constant_dynamic-slice_fusion.1
  15.4 2.1 constant_dynamic-slice_fusion
  17.5 1.3 collective-permute-done.6
  18.8 0.7 copy-done.13
  19.5 1.8 pick.1
  21.2 0.0 all-gather.7.cloned.1.call-update
  21.3 0.0 collective-permute-done.dt_oth
  21.3 67.4 %all-gather.5.cloned.1.call-done = bf16[9216,1024]{1,0:T(8,128)(2,1)} async-done(((bf16[288,1024]{1,0:T(8,128)(2,1)}), bf16[9216,1024]{1,0:T(8,128)(2,1)}) %all-gather.5.cloned.1.call-update) | async-done | bytes 18874384 | tf_op jit(solution)/shard_map/all_gather | solution.py:219
  88.7 5.3 %scores.2 = (f32[2,192,1024]{2,1,0:T(8,128)}, bf16[2,192,1024]{2,1,0:T(8,128)(2,1)}) custom-call(s32[4]{0:T(128)} %pad_add_fusion.info, bf16[192,1024]{1,0:T(8,128)(2,1)} %get-tuple-element.35.emb, bf16[2,512,512]{2,1,0:T(8,128)(2,1)} %bitcast.36, bf16[2,512,512]{2,1,0:T(8,128)(2,1)} %copy-done.1, bf16[2,16,288,1024]{3,2,1,0:T(8,128)(2,1)} %bitcast.17), custom_call_target="tpu_custom_call" | custom-call | flops 99999997952 | bytes 1024 | tf_op jit(solution)/shard_map/scores/pallas_call | solution.py:259
  94.0 1.6 collective-permute-start.4
  95.6 1.3 collective-permute-start.1
  96.8 5.4 %scores.3 = (f32[2,192,1024]{2,1,0:T(8,128)}, bf16[2,192,1024]{2,1,0:T(8,128)(2,1)}) custom-call(s32[4]{0:T(128)} %pad_add_fusion.info, bf16[192,1024]{1,0:T(8,128)(2,1)} %get-tuple-element.22.emb, bf16[2,512,512]{2,1,0:T(8,128)(2,1)} %bitcast.37, bf16[2,512,512]{2,1,0:T(8,128)(2,1)} %copy-done.1, bf16[2,16,288,1024]{3,2,1,0:T(8,128)(2,1)} %bitcast.18), custom_call_target="tpu_custom_call" | custom-call | flops 99999997952 | bytes 1024 | tf_op jit(solution)/shard_map/scores/pallas_call | solution.py:259
  102.2 0.7 collective-permute-start.3
  102.9 1.3 collective-permute-start.9
  104.2 0.0 collective-permute-done.4.a
  104.3 14.6 %collective-permute-done.1.to_3 = bf16[2,192,1024]{2,1,0:T(8,128)(2,1)} collective-permute-done((bf16[2,192,1024]{2,1,0:T(8,128)(2,1)}, bf16[2,192,1024]{2,1,0:T(8,128)(2,1)}, u32[]{:S(2)}, u32[]{:S(2)}) %collective-permute-start.1) | collective-permute-done | bytes 786464 | tf_op jit(solution)/shard_map/ppermute | solution.py:210
  118.8 1.3 collective-permute-start.2
  120.2 1.6 finish1.2.own.refs_2_
  121.8 0.7 collective-permute-start.5
  122.5 0.0 collective-permute-done.3.a
  122.6 0.9 copy-done.11
  123.5 12.2 %collective-permute-done.9.to_3 = bf16[2,192,1024]{2,1,0:T(8,128)(2,1)S(1)} collective-permute-done((bf16[2,192,1024]{2,1,0:T(8,128)(2,1)}, bf16[2,192,1024]{2,1,0:T(8,128)(2,1)S(1)}, u32[]{:S(2)}, u32[]{:S(2)}) %collective-permute-start.9) | collective-permute-done | bytes 786464 | tf_op jit(solution)/shard_map/ppermute | solution.py:210
  135.7 1.3 collective-permute-start.10
  137.0 1.7 finish1.3.own.refs_2_
  138.7 1.5 collective-permute-start.11
  140.3 0.0 collective-permute-done.2.to_2
  140.3 0.9 copy-done.5
  141.1 8.1 %update.2.r = f32[2,192,1024]{2,1,0:T(8,128)} custom-call(s32[4]{0:T(128)} %pad_add_fusion.info, bf16[2,16,288,1024]{3,2,1,0:T(8,128)(2,1)} %bitcast.23, f32[2,192,1024]{2,1,0:T(8,128)} %hold.1.r, bf16[2,192,1024]{2,1,0:T(8,128)(2,1)} %collective-permute-done.1.to_3, bf16[2,192,1024]{2,1,0:T(8,128)(2,1)} %copy-done.5), custom_call_target="tpu_custom_call" | custom-call | bytes 1024 | tf_op jit(solution)/shard_map/update/pallas_call | solution.py:316
  149.3 0.0 all-gather.7.cloned.1.call-done
  149.3 1.6 partial.2
  150.9 1.3 collective-permute-start.8
  152.2 0.0 collective-permute-done.5.a
  152.2 0.9 copy-done.8
  153.1 1.7 finish2.2.refs_3_
  154.8 1.3 collective-permute-start.7
  156.1 0.0 collective-permute-done.10.to_2
  156.1 0.9 copy-done.4
  157.0 7.9 %update.3.r = f32[2,192,1024]{2,1,0:T(8,128)} custom-call(s32[4]{0:T(128)} %pad_add_fusion.info, bf16[2,16,288,1024]{3,2,1,0:T(8,128)(2,1)} %bitcast.25, f32[2,192,1024]{2,1,0:T(8,128)} %get-tuple-element.24.r, bf16[2,192,1024]{2,1,0:T(8,128)(2,1)} %copy-done.3, bf16[2,192,1024]{2,1,0:T(8,128)(2,1)} %copy-done.4), custom_call_target="tpu_custom_call" | custom-call | bytes 1024 | tf_op jit(solution)/shard_map/update/pallas_call | solution.py:316
  164.9 1.6 finish2.3.refs_3_
  166.6 1.3 collective-permute-start.12
  167.9 1.8 partial.3
  169.7 1.3 collective-permute-start.13
  171.0 7.9 %collective-permute-done.7.a = bf16[2,192,1024]{2,1,0:T(8,128)(2,1)S(1)} collective-permute-done((bf16[2,192,1024]{2,1,0:T(8,128)(2,1)}, bf16[2,192,1024]{2,1,0:T(8,128)(2,1)S(1)}, u32[]{:S(2)}, u32[]{:S(2)}) %collective-permute-start.7) | collective-permute-done | bytes 786464 | tf_op jit(solution)/shard_map/ppermute | solution.py:210
  179.0 0.9 copy-done.9
  179.8 0.9 copy-done.6
  180.7 11.4 %finish3.2 = (bf16[192,1024]{1,0:T(8,128)(2,1)}, bf16[192,1024]{1,0:T(8,128)(2,1)}) custom-call(s32[4]{0:T(128)} %pad_add_fusion.info, f32[2,192,1024]{2,1,0:T(8,128)} %update.2.r, bf16[2,192,1024]{2,1,0:T(8,128)(2,1)} %copy-done.9, bf16[2,16,288,1024]{3,2,1,0:T(8,128)(2,1)} %bitcast.27, bf16[2,512,512]{2,1,0:T(8,128)(2,1)} %bitcast.42, ...), custom_call_target="tpu_custom_call" | custom-call | flops 800000000 | bytes 1024 | tf_op jit(solution)/shard_map/finish3/pallas_call | solution.py:289
  192.1 7.1 %collective-permute-done.12.a = bf16[2,192,1024]{2,1,0:T(8,128)(2,1)S(1)} collective-permute-done((bf16[2,192,1024]{2,1,0:T(8,128)(2,1)}, bf16[2,192,1024]{2,1,0:T(8,128)(2,1)S(1)}, u32[]{:S(2)}, u32[]{:S(2)}) %collective-permute-start.12) | collective-permute-done | bytes 786464 | tf_op jit(solution)/shard_map/ppermute | solution.py:210
  199.3 0.9 copy-done.7
  200.2 0.9 copy-done.10
  201.1 11.5 %finish3.3 = (bf16[192,1024]{1,0:T(8,128)(2,1)}, bf16[192,1024]{1,0:T(8,128)(2,1)}) custom-call(s32[4]{0:T(128)} %pad_add_fusion.info, f32[2,192,1024]{2,1,0:T(8,128)} %update.3.r, bf16[2,192,1024]{2,1,0:T(8,128)(2,1)} %copy-done.7, bf16[2,16,288,1024]{3,2,1,0:T(8,128)(2,1)} %bitcast.28, bf16[2,512,512]{2,1,0:T(8,128)(2,1)} %bitcast.43, ...), custom_call_target="tpu_custom_call" | custom-call | flops 800000000 | bytes 1024 | tf_op jit(solution)/shard_map/finish3/pallas_call | solution.py:289
  212.6 2.4 %collective-permute-start.15 = (bf16[192,1024]{1,0:T(8,128)(2,1)}, bf16[192,1024]{1,0:T(8,128)(2,1)S(1)}, u32[]{:S(2)}, u32[]{:S(2)}) collective-permute-start(bf16[192,1024]{1,0:T(8,128)(2,1)} %get-tuple-element.34), channel_id=1, source_target_pairs={{0,1},{1,0},{2,3},{3,2},{4,5},{5,4},{6,7},{7,6},{8,9},{9,8},{10,11... | collective-permute-start | bytes 1179656 | tf_op jit(solution)/shard_map/ppermute | solution.py:213
  215.0 0.1 collective-permute-start.14
  215.1 1.5 collective-permute-done.15
  216.5 0.4 collective-permute-done.14
  216.9 2.6 %maximum_select_fusion = bf16[768,1024]{1,0:T(8,128)(2,1)} fusion(bf16[192,1024]{1,0:T(8,128)(2,1)S(1)} %collective-permute-done.15, bf16[192,1024]{1,0:T(8,128)(2,1)S(1)} %collective-permute-done.14, bf16[192,1024]{1,0:T(8,128)(2,1)} %get-tuple-element.32, bf16[192,1024]{1,0:T(8,128)(2,1)S(1)} %copy-done.12, pred[]{:T(512)S(6)} %eq.6), kind=kLoop, calls=%fused_computation | loop fusion | flops 13369344 | bytes 3145729 | tf_op jit(solution)/shard_map/jit(_where)/select_n | solution.py:346
  (28 shorter events, 0.1 us)
Async XLA Ops:
  6.5 2.1 copy-start.14
  6.5 82.1 %all-gather.5.cloned.1.call-start = ((), (), s32[]{:S(2)}) async-start(), calls=%async_computation | async-start | bytes 19464192 | tf_op jit(solution)/shard_map/all_gather | solution.py:219
  6.5 3.1 %copy-start.2 = (bf16[2,512,512]{2,1,0:T(8,128)(2,1)S(1)}, bf16[2,512,512]{2,1,0:T(8,128)(2,1)}, u32[]{:S(2)}) copy-start(bf16[2,512,512]{2,1,0:T(8,128)(2,1)} %param.7) | copy-start | bytes 3145732
  9.5 139.7 %all-gather.7.cloned.1.call-start = ((), (), s32[]{:S(2)}) async-start(), calls=%async_computation.1 | async-start | bytes 8650752 | tf_op jit(solution)/shard_map/all_gather | solution.py:219
  10.2 11.1 %copy-start = (bf16[2,512,512]{1,2,0:T(8,128)(2,1)}, bf16[2,512,512]{1,2,0:T(8,128)(2,1)S(1)}, u32[]{:S(2)}) copy-start(bf16[2,512,512]{1,2,0:T(8,128)(2,1)S(1)} %copy.6) | copy-start | bytes 3145732
  10.2 11.1 %collective-permute-start = (bf16[2,512,512]{2,1,0:T(8,128)(2,1)S(1)}, bf16[2,512,512]{2,1,0:T(8,128)(2,1)S(1)}, u32[]{:S(2)}, u32[]{:S(2)}) collective-permute-start(bf16[2,512,512]{2,1,0:T(8,128)(2,1)S(1)} %bitcast.35), channel_id=1, source_target_pairs={{0,1},{1,0},{2,3},{3,2},{4,5},{5,4},{6,7},{7,6},{8,9},{9,8},{10,11... | collective-permute-start | bytes 3145736 | tf_op jit(solution)/shard_map/ppermute | solution.py:213
  10.9 7.9 %collective-permute-start.6 = (bf16[4,32,1024]{2,1,0:T(8,128)(2,1)S(1)}, bf16[4,32,1024]{2,1,0:T(8,128)(2,1)S(1)}, u32[]{:S(2)}, u32[]{:S(2)}) collective-permute-start(bf16[4,32,1024]{2,1,0:T(8,128)(2,1)S(1)} %get-tuple-element.37), channel_id=1, source_target_pairs={{6,2},{7,3},{14,10},{15,11},{22,18},{23,19},{30,26},{31,27},{38,34... | collective-permute-start | bytes 786440 | tf_op jit(solution)/shard_map/ppermute | solution.py:210
  18.8 0.7 copy-start.13
  21.3 67.4 %copy-start.1 = (bf16[2,512,512]{2,1,0:T(8,128)(2,1)}, bf16[2,512,512]{2,1,0:T(8,128)(2,1)S(1)}, u32[]{:S(2)}) copy-start(bf16[2,512,512]{2,1,0:T(8,128)(2,1)S(1)} %collective-permute-done.dt_oth) | copy-start | bytes 3145732
  94.0 10.3 %collective-permute-start.4 = (bf16[2,192,1024]{2,1,0:T(8,128)(2,1)}, bf16[2,192,1024]{2,1,0:T(8,128)(2,1)}, u32[]{:S(2)}, u32[]{:S(2)}) collective-permute-start(bf16[2,192,1024]{2,1,0:T(8,128)(2,1)} %get-tuple-element.21.refs_1_), channel_id=1, source_target_pairs={{0,2},{1,3},{8,10},{9,11},{16,18},{17,19},{24,26},{25,27},{32,34},... | collective-permute-start | bytes 2359304 | tf_op jit(solution)/shard_map/ppermute | solution.py:210
  95.6 23.3 %collective-permute-start.1 = (bf16[2,192,1024]{2,1,0:T(8,128)(2,1)}, bf16[2,192,1024]{2,1,0:T(8,128)(2,1)}, u32[]{:S(2)}, u32[]{:S(2)}) collective-permute-start(bf16[2,192,1024]{2,1,0:T(8,128)(2,1)} %get-tuple-element.21.refs_1_), channel_id=1, source_target_pairs={{0,6},{1,7},{8,14},{9,15},{16,22},{17,23},{24,30},{25,31},{32,38},... | collective-permute-start | bytes 2359304 | tf_op jit(solution)/shard_map/ppermute | solution.py:210
  102.2 20.3 %collective-permute-start.3 = (bf16[2,192,1024]{2,1,0:T(8,128)(2,1)}, bf16[2,192,1024]{2,1,0:T(8,128)(2,1)S(1)}, u32[]{:S(2)}, u32[]{:S(2)}) collective-permute-start(bf16[2,192,1024]{2,1,0:T(8,128)(2,1)} %get-tuple-element.23.token.refs_1_), channel_id=1, source_target_pairs={{0,2},{1,3},{8,10},{9,11},{16,18},{17,19},{24,26},{25,27},{32,34},... | collective-permute-start | bytes 2359304 | tf_op jit(solution)/shard_map/ppermute | solution.py:210
  102.9 32.8 %collective-permute-start.9 = (bf16[2,192,1024]{2,1,0:T(8,128)(2,1)}, bf16[2,192,1024]{2,1,0:T(8,128)(2,1)S(1)}, u32[]{:S(2)}, u32[]{:S(2)}) collective-permute-start(bf16[2,192,1024]{2,1,0:T(8,128)(2,1)} %get-tuple-element.23.token.refs_1_), channel_id=1, source_target_pairs={{0,6},{1,7},{8,14},{9,15},{16,22},{17,23},{24,30},{25,31},{32,38},... | collective-permute-start | bytes 2359304 | tf_op jit(solution)/shard_map/ppermute | solution.py:210
  118.8 21.4 %collective-permute-start.2 = (bf16[2,192,1024]{2,1,0:T(8,128)(2,1)}, bf16[2,192,1024]{2,1,0:T(8,128)(2,1)S(1)}, u32[]{:S(2)}, u32[]{:S(2)}) collective-permute-start(bf16[2,192,1024]{2,1,0:T(8,128)(2,1)} %collective-permute-done.1.to_3), channel_id=1, source_target_pairs={{6,4},{7,5},{14,12},{15,13},{22,20},{23,21},{30,28},{31,29},{38,36... | collective-permute-start | bytes 2359304 | tf_op jit(solution)/shard_map/ppermute | solution.py:210
  121.8 30.4 %collective-permute-start.5 = (bf16[2,192,1024]{2,1,0:T(8,128)(2,1)}, bf16[2,192,1024]{2,1,0:T(8,128)(2,1)S(1)}, u32[]{:S(2)}, u32[]{:S(2)}) collective-permute-start(bf16[2,192,1024]{2,1,0:T(8,128)(2,1)} %finish1.2.own.refs_2_), channel_id=1, source_target_pairs={{2,4},{3,5},{10,12},{11,13},{18,20},{19,21},{26,28},{27,29},{34,36... | collective-permute-start | bytes 2359304 | tf_op jit(solution)/shard_map/ppermute | solution.py:210
  122.6 0.9 copy-start.11
  135.7 3.0 %copy-start.3 = (bf16[2,192,1024]{2,1,0:T(8,128)(2,1)}, bf16[2,192,1024]{2,1,0:T(8,128)(2,1)S(1)}, u32[]{:S(2)}) copy-start(bf16[2,192,1024]{2,1,0:T(8,128)(2,1)S(1)} %collective-permute-done.9.to_3) | copy-start | bytes 2359300
  135.7 20.4 %collective-permute-start.10 = (bf16[2,192,1024]{2,1,0:T(8,128)(2,1)S(1)}, bf16[2,192,1024]{2,1,0:T(8,128)(2,1)S(1)}, u32[]{:S(2)}, u32[]{:S(2)}) collective-permute-start(bf16[2,192,1024]{2,1,0:T(8,128)(2,1)S(1)} %collective-permute-done.9.to_3), channel_id=1, source_target_pairs={{6,4},{7,5},{14,12},{15,13},{22,20},{23,21},{30,28},{31,29},{38,36... | collective-permute-start | bytes 2359304 | tf_op jit(solution)/shard_map/ppermute | solution.py:210
  138.7 26.2 %collective-permute-start.11 = (bf16[2,192,1024]{2,1,0:T(8,128)(2,1)}, bf16[2,192,1024]{2,1,0:T(8,128)(2,1)}, u32[]{:S(2)}, u32[]{:S(2)}) collective-permute-start(bf16[2,192,1024]{2,1,0:T(8,128)(2,1)} %finish1.3.own.refs_2_), channel_id=1, source_target_pairs={{2,4},{3,5},{10,12},{11,13},{18,20},{19,21},{26,28},{27,29},{34,36... | collective-permute-start | bytes 2359304 | tf_op jit(solution)/shard_map/ppermute | solution.py:210
  140.3 0.9 copy-start.5
  150.9 28.0 %collective-permute-start.8 = (bf16[2,192,1024]{2,1,0:T(8,128)(2,1)}, bf16[2,192,1024]{2,1,0:T(8,128)(2,1)S(1)}, u32[]{:S(2)}, u32[]{:S(2)}) collective-permute-start(bf16[2,192,1024]{2,1,0:T(8,128)(2,1)} %partial.2), channel_id=1, source_target_pairs={{2,6},{3,7},{10,14},{11,15},{18,22},{19,23},{26,30},{27,31},{34,38... | collective-permute-start | bytes 2359304 | tf_op jit(solution)/shard_map/ppermute | solution.py:210
  152.2 0.9 copy-start.8
  154.8 24.2 %collective-permute-start.7 = (bf16[2,192,1024]{2,1,0:T(8,128)(2,1)}, bf16[2,192,1024]{2,1,0:T(8,128)(2,1)S(1)}, u32[]{:S(2)}, u32[]{:S(2)}) collective-permute-start(bf16[2,192,1024]{2,1,0:T(8,128)(2,1)} %finish2.2.refs_3_), channel_id=1, source_target_pairs={{4,6},{5,7},{12,14},{13,15},{20,22},{21,23},{28,30},{29,31},{36,38... | collective-permute-start | bytes 2359304 | tf_op jit(solution)/shard_map/ppermute | solution.py:210
  156.1 0.9 copy-start.4
  166.6 32.7 %collective-permute-start.12 = (bf16[2,192,1024]{2,1,0:T(8,128)(2,1)}, bf16[2,192,1024]{2,1,0:T(8,128)(2,1)S(1)}, u32[]{:S(2)}, u32[]{:S(2)}) collective-permute-start(bf16[2,192,1024]{2,1,0:T(8,128)(2,1)} %finish2.3.refs_3_), channel_id=1, source_target_pairs={{4,6},{5,7},{12,14},{13,15},{20,22},{21,23},{28,30},{29,31},{36,38... | collective-permute-start | bytes 2359304 | tf_op jit(solution)/shard_map/ppermute | solution.py:210
  169.7 29.6 %collective-permute-start.13 = (bf16[2,192,1024]{2,1,0:T(8,128)(2,1)}, bf16[2,192,1024]{2,1,0:T(8,128)(2,1)S(1)}, u32[]{:S(2)}, u32[]{:S(2)}) collective-permute-start(bf16[2,192,1024]{2,1,0:T(8,128)(2,1)} %partial.3), channel_id=1, source_target_pairs={{2,6},{3,7},{10,14},{11,15},{18,22},{19,23},{26,30},{27,31},{34,38... | collective-permute-start | bytes 2359304 | tf_op jit(solution)/shard_map/ppermute | solution.py:210
  179.0 0.9 copy-start.9
  179.8 0.9 copy-start.6
  199.3 0.9 copy-start.7
  199.3 15.7 %copy-start.15 = (bf16[192,1024]{1,0:T(8,128)(2,1)S(1)}, bf16[192,1024]{1,0:T(8,128)(2,1)}, u32[]{:S(2)}) copy-start(bf16[192,1024]{1,0:T(8,128)(2,1)} %get-tuple-element.33) | copy-start | bytes 1179652
  199.3 17.6 %copy-start.12 = (bf16[192,1024]{1,0:T(8,128)(2,1)S(1)}, bf16[192,1024]{1,0:T(8,128)(2,1)}, u32[]{:S(2)}) copy-start(bf16[192,1024]{1,0:T(8,128)(2,1)} %get-tuple-element.28) | copy-start | bytes 1179652
  200.2 0.9 copy-start.10
  212.6 3.9 %collective-permute-start.15 = (bf16[192,1024]{1,0:T(8,128)(2,1)}, bf16[192,1024]{1,0:T(8,128)(2,1)S(1)}, u32[]{:S(2)}, u32[]{:S(2)}) collective-permute-start(bf16[192,1024]{1,0:T(8,128)(2,1)} %get-tuple-element.34), channel_id=1, source_target_pairs={{0,1},{1,0},{2,3},{3,2},{4,5},{5,4},{6,7},{7,6},{8,9},{9,8},{10,11... | collective-permute-start | bytes 1179656 | tf_op jit(solution)/shard_map/ppermute | solution.py:213
  215.0 1.9 collective-permute-start.14
Sparse Core Ops, SparseCore 0:
  9.7 78.9 all-gather.4
  91.0 52.2 all-gather.6
